TPU v7x, 256 devices: a whole 4x4x8 slice. The times are simulated.
256 devices in a mesh: ctx: 32 (over z_lo, x, core), exp: 8 (over y, z_hi).
Axes of the slice: x: 4, y: 4, z: 8 (z_hi: 2, z_lo: 4; z = z_hi * 4 + z_lo), core: 2. Of those that a mesh axis runs over, the one named last changes fastest.
Arguments:
- queries: bfloat16 [4096, 8192], P('ctx', 'exp'), may hold values from -6 to 6
- grad_heads: bfloat16 [4096, 8192], P('ctx', 'exp'), may hold values from -6 to 6
- latents: bfloat16 [4096, 512], P('ctx'), may hold values from -48 to 48
- w_uk: bfloat16 [512, 8192], P('ctx', 'exp'), may hold values from -0.25 to 0.25
- w_uv: bfloat16 [512, 8192], P('ctx', 'exp'), may hold values from -0.25 to 0.25
- moe_in: bfloat16 [4096, 7168], P('ctx', 'exp'), may hold values from -6 to 6
- grad_out: bfloat16 [4096, 7168], P('ctx', 'exp'), may hold values from -6 to 6
- routes: int32 [4096, 8], P('ctx'), may hold values from 0 to 255, as said below
- slots: int32 [4096, 8], P('ctx'), may hold values from -1 to 1, as said below
- gates: bfloat16 [4096, 8], P('ctx'), may hold values from 0.099609375 to 1
- w_gate: bfloat16 [32, 7168, 1024], P('ctx', None, 'exp'), may hold values from -0.0625 to 0.0625
- w_up: bfloat16 [32, 7168, 1024], P('ctx', None, 'exp'), may hold values from -0.0625 to 0.0625
- w_down: bfloat16 [32, 1024, 7168], P('ctx', 'exp'), may hold values from -0.1875 to 0.1875
Outputs:
- d_queries: bfloat16 [4096, 8192], P('ctx', 'exp')
- d_latents: float32 [4096, 512], P('ctx', 'exp')
- grad_w_uk: float32 [512, 8192], P('ctx', 'exp')
- grad_w_uv: float32 [512, 8192], P('ctx', 'exp')
- moe_grad: bfloat16 [4096, 7168], P('ctx', 'exp')
- gate_grads: float32 [4096, 8], P('ctx')
- grad_w_gate: bfloat16 [32, 7168, 1024], P('ctx', None, 'exp')
- grad_w_up: bfloat16 [32, 7168, 1024], P('ctx', None, 'exp')
- grad_w_down: bfloat16 [32, 1024, 7168], P('ctx', 'exp')
Inputs may be any that keep to these rules, and one draw needn't show every extreme that they name: `routes`: each row names 8 different experts. One expert below 32 is named by every row. `slots`: for a route to an expert below 32: the number of earlier rows of the same aligned block of 128 rows (one device's tokens) that name that expert, if it is below 2; -1 otherwise and for routes to experts of 32 or above.
All inputs are finite; a program needn't handle non-finite values.
Results may differ from a plain program's by a relative error of at most 0.0085.
The roundings to bfloat16 on the way count: a program that leaves them out, or rounds other values in their place, can miss the bound.
Values may be sent and summed in bfloat16 or wider, within the bound.
A program may use at most 320 MiB of HBM per device.

v0:
```python
import jax
import jax.numpy as jnp
from jax import lax
from jax.sharding import PartitionSpec as P

HD = 128
CAP = 2


def attention_backward(queries, grad_heads, latents, w_uk, w_uv):
    tok_count = queries.shape[0]
    latent_all, key_weight, value_weight = (
        lax.all_gather(latents, "ctx", axis=0, tiled=True),
        lax.all_gather(w_uk, "ctx", axis=0, tiled=True),
        lax.all_gather(w_uv, "ctx", axis=0, tiled=True),
    )
    key_count, latent_width = latent_all.shape
    head_count = key_weight.shape[1] // HD
    query_split = queries.reshape(tok_count, head_count, HD)
    grad_split = grad_heads.reshape(tok_count, head_count, HD)
    key_split = key_weight.reshape(latent_width, head_count, HD)
    value_split = value_weight.reshape(latent_width, head_count, HD)
    row_count = head_count * tok_count
    query_latent = (
        jnp.einsum("thd,khd->htk", query_split, key_split, preferred_element_type=jnp.float32)
        .astype(jnp.bfloat16)
        .reshape(row_count, latent_width)
    )
    grad_latent = (
        jnp.einsum("thd,khd->htk", grad_split, value_split, preferred_element_type=jnp.float32)
        .astype(jnp.bfloat16)
        .reshape(row_count, latent_width)
    )
    scale_factor = HD ** (-0.5)
    key_block = min(key_count, 256)
    block_count = key_count // key_block
    first_query = lax.axis_index("ctx") * tok_count
    query_position = first_query + jnp.arange(row_count, dtype=jnp.int32) % tok_count
    last_query = first_query + tok_count - 1

    def visible(block_index):
        return block_index * key_block <= last_query

    def key_rows(block_index):
        return lax.dynamic_slice_in_dim(latent_all, block_index * key_block, key_block, 0)

    def score_step(block_index, scores):

        def compute_block(current):
            raw_scores = (
                lax.dot_general(
                    query_latent,
                    key_rows(block_index),
                    (((1,), (1,)), ((), ())),
                    preferred_element_type=jnp.float32,
                )
                * scale_factor
            )
            key_position = block_index * key_block + jnp.arange(key_block, dtype=jnp.int32)
            masked = jnp.where(
                key_position[None, :] <= query_position[:, None], raw_scores, -jnp.inf
            )
            return lax.dynamic_update_slice_in_dim(current, masked, block_index * key_block, 1)

        return lax.cond(visible(block_index), compute_block, lambda current: current, scores)

    scores = lax.fori_loop(
        0, block_count, score_step, jnp.full((row_count, key_count), -jnp.inf, jnp.float32)
    )
    top_score = jnp.max(scores, axis=1, keepdims=True)
    log_total = top_score + jnp.log(jnp.sum(jnp.exp(scores - top_score), axis=1, keepdims=True))

    def prob_block(block_index):
        return jnp.exp(
            lax.dynamic_slice_in_dim(scores, block_index * key_block, key_block, 1) - log_total
        )

    def output_step(block_index, running):

        def output_accumulate(current):
            return current + jnp.dot(
                prob_block(block_index).astype(jnp.bfloat16),
                key_rows(block_index),
                preferred_element_type=jnp.float32,
            )

        return lax.cond(visible(block_index), output_accumulate, lambda current: current, running)

    output_latent = lax.fori_loop(
        0, block_count, output_step, jnp.zeros((row_count, latent_width), jnp.float32)
    )
    delta_sum = jnp.sum(grad_latent.astype(jnp.float32) * output_latent, axis=1, keepdims=True)

    def gradient_step(block_index, carried):

        def gradient_accumulate(running_state):
            dq_running, latent_grads = running_state
            keys_here = key_rows(block_index)
            prob_values = prob_block(block_index)
            probs_low = prob_values.astype(jnp.bfloat16)
            d_prob = lax.dot_general(
                grad_latent, keys_here, (((1,), (1,)), ((), ())), preferred_element_type=jnp.float32
            )
            d_score = (prob_values * (d_prob - delta_sum) * scale_factor).astype(jnp.bfloat16)
            dq_running = dq_running + jnp.dot(
                d_score, keys_here, preferred_element_type=jnp.float32
            )
            block_grad = lax.dot_general(
                d_score, query_latent, (((0,), (0,)), ((), ())), preferred_element_type=jnp.float32
            )
            block_grad = block_grad + lax.dot_general(
                probs_low, grad_latent, (((0,), (0,)), ((), ())), preferred_element_type=jnp.float32
            )
            latent_grads = lax.dynamic_update_slice_in_dim(
                latent_grads, block_grad, block_index * key_block, 0
            )
            return (dq_running, latent_grads)

        return lax.cond(
            visible(block_index), gradient_accumulate, lambda running_state: running_state, carried
        )

    dq_running, latent_grads = lax.fori_loop(
        0,
        block_count,
        gradient_step,
        (
            jnp.zeros((row_count, latent_width), jnp.float32),
            jnp.zeros((key_count, latent_width), jnp.float32),
        ),
    )
    dq_low = dq_running.astype(jnp.bfloat16).reshape(head_count, tok_count, latent_width)
    d_queries = (
        jnp.einsum("htk,khd->thd", dq_low, key_split, preferred_element_type=jnp.float32)
        .astype(jnp.bfloat16)
        .reshape(tok_count, head_count * HD)
    )
    key_grads = jnp.einsum(
        "htk,thd->khd", dq_low, query_split, preferred_element_type=jnp.float32
    ).reshape(latent_width, head_count * HD)
    output_low = output_latent.astype(jnp.bfloat16).reshape(head_count, tok_count, latent_width)
    value_grads = jnp.einsum(
        "htk,thd->khd", output_low, grad_split, preferred_element_type=jnp.float32
    ).reshape(latent_width, head_count * HD)
    latent_part, key_summed, value_summed = (
        lax.psum_scatter(latent_grads, "ctx", scatter_dimension=0, tiled=True),
        lax.psum_scatter(key_grads, "ctx", scatter_dimension=0, tiled=True),
        lax.psum_scatter(value_grads, "ctx", scatter_dimension=0, tiled=True),
    )
    d_latents = lax.psum_scatter(latent_part, "exp", scatter_dimension=1, tiled=True)
    return (d_queries, d_latents, key_summed, value_summed)


def expert_backward(moe_in, grad_out, routes, slots, gates, w_gate, w_up, w_down):
    tok_count, slice_width = moe_in.shape
    expert_count = lax.axis_size("ctx")
    slot_count = expert_count * CAP
    destination = jnp.where(slots >= 0, routes * CAP + slots, -1)
    matches = (
        destination[:, :, None] == jnp.arange(slot_count, dtype=jnp.int32)[None, None, :]
    ).astype(jnp.float32)
    selector = jnp.sum(matches, axis=1)
    selector_low = selector.astype(jnp.bfloat16)
    rows_send = lax.dot_general(
        selector_low, moe_in, (((0,), (0,)), ((), ())), preferred_element_type=jnp.float32
    ).astype(jnp.bfloat16)
    grads_send = lax.dot_general(
        selector_low, grad_out, (((0,), (0,)), ((), ())), preferred_element_type=jnp.float32
    ).astype(jnp.bfloat16)
    gate_send = jnp.einsum(
        "tjp,tj->p", matches, gates.astype(jnp.float32), precision=lax.Precision.HIGHEST
    ).astype(jnp.bfloat16)
    rows_recv, grads_recv, gate_recv = (
        lax.all_to_all(
            rows_send.reshape(expert_count, CAP, slice_width),
            "ctx",
            split_axis=0,
            concat_axis=0,
            tiled=True,
        ),
        lax.all_to_all(
            grads_send.reshape(expert_count, CAP, slice_width),
            "ctx",
            split_axis=0,
            concat_axis=0,
            tiled=True,
        ),
        lax.all_to_all(
            gate_send.reshape(expert_count, CAP), "ctx", split_axis=0, concat_axis=0, tiled=True
        ),
    )
    rows_full, grads_full = (
        lax.all_gather(rows_recv, "exp", axis=2, tiled=True),
        lax.all_gather(grads_recv, "exp", axis=2, tiled=True),
    )
    model_width = rows_full.shape[2]
    rows_flat = rows_full.reshape(slot_count, model_width)
    grads_flat = grads_full.reshape(slot_count, model_width)
    gate_column = gate_recv.reshape(slot_count, 1).astype(jnp.float32)
    gate_weight = w_gate[0]
    up_weight = w_up[0]
    down_weight = w_down[0]
    hidden_gate = jnp.dot(rows_flat, gate_weight, preferred_element_type=jnp.float32)
    hidden_up = jnp.dot(rows_flat, up_weight, preferred_element_type=jnp.float32)
    sigmoid_gate = jax.nn.sigmoid(hidden_gate)
    activation = hidden_gate * sigmoid_gate * hidden_up
    act_grad = lax.dot_general(
        grads_flat, down_weight, (((1,), (1,)), ((), ())), preferred_element_type=jnp.float32
    )
    gate_summed = lax.psum(jnp.sum(act_grad * activation, axis=1), "exp")
    scaled_grad = gate_column * act_grad
    scaled_act = (gate_column * activation).astype(jnp.bfloat16)
    down_grad = lax.dot_general(
        scaled_act, grads_flat, (((0,), (0,)), ((), ())), preferred_element_type=jnp.float32
    ).astype(jnp.bfloat16)
    grad_gate_in = (
        scaled_grad * hidden_up * sigmoid_gate * (1.0 + hidden_gate * (1.0 - sigmoid_gate))
    ).astype(jnp.bfloat16)
    grad_up_in = (scaled_grad * hidden_gate * sigmoid_gate).astype(jnp.bfloat16)
    gate_wgrad = lax.dot_general(
        rows_flat, grad_gate_in, (((0,), (0,)), ((), ())), preferred_element_type=jnp.float32
    ).astype(jnp.bfloat16)
    up_wgrad = lax.dot_general(
        rows_flat, grad_up_in, (((0,), (0,)), ((), ())), preferred_element_type=jnp.float32
    ).astype(jnp.bfloat16)
    row_grads = lax.dot_general(
        grad_gate_in, gate_weight, (((1,), (1,)), ((), ())), preferred_element_type=jnp.float32
    )
    row_grads = row_grads + lax.dot_general(
        grad_up_in, up_weight, (((1,), (1,)), ((), ())), preferred_element_type=jnp.float32
    )
    gate_back_in = gate_summed.reshape(expert_count, CAP)
    returned, gate_back = (
        lax.all_to_all(
            row_grads.reshape(expert_count, CAP, model_width),
            "ctx",
            split_axis=0,
            concat_axis=0,
            tiled=True,
        ),
        lax.all_to_all(gate_back_in, "ctx", split_axis=0, concat_axis=0, tiled=True),
    )
    combined = jnp.dot(
        selector, returned.reshape(slot_count, model_width), precision=lax.Precision.HIGHEST
    )
    moe_grad = lax.psum_scatter(combined, "exp", scatter_dimension=1, tiled=True).astype(
        jnp.bfloat16
    )
    gate_grads = jnp.einsum(
        "tjp,p->tj", matches, gate_back.reshape(slot_count), precision=lax.Precision.HIGHEST
    )
    return (moe_grad, gate_grads, gate_wgrad[None], up_wgrad[None], down_grad[None])


def on_device(
    queries,
    grad_heads,
    latents,
    w_uk,
    w_uv,
    moe_in,
    grad_out,
    routes,
    slots,
    gates,
    w_gate,
    w_up,
    w_down,
):
    d_queries, d_latents, key_summed, value_summed = attention_backward(
        queries, grad_heads, latents, w_uk, w_uv
    )
    moe_grad, gate_grads, gate_wgrad, up_wgrad, down_grad = expert_backward(
        moe_in, grad_out, routes, slots, gates, w_gate, w_up, w_down
    )
    return (
        d_queries,
        d_latents,
        key_summed,
        value_summed,
        moe_grad,
        gate_grads,
        gate_wgrad,
        up_wgrad,
        down_grad,
    )


def solution(mesh):
    in_specs = (
        P("ctx", "exp"),
        P("ctx", "exp"),
        P("ctx", None),
        P("ctx", "exp"),
        P("ctx", "exp"),
        P("ctx", "exp"),
        P("ctx", "exp"),
        P("ctx", None),
        P("ctx", None),
        P("ctx", None),
        P("ctx", None, "exp"),
        P("ctx", None, "exp"),
        P("ctx", "exp", None),
    )
    out_specs = (
        P("ctx", "exp"),
        P("ctx", "exp"),
        P("ctx", "exp"),
        P("ctx", "exp"),
        P("ctx", "exp"),
        P("ctx", None),
        P("ctx", None, "exp"),
        P("ctx", None, "exp"),
        P("ctx", "exp", None),
    )
    return jax.shard_map(
        on_device, mesh=mesh, in_specs=in_specs, out_specs=out_specs, check_vma=False
    )
```

profile of v0, /device:TPU:8, one launch (start us, length us, event | category | flops | bytes accessed | tf_op | source)
XLA Modules:
  0.0 1223.2 jit_solution(16969518358349504228)
XLA Ops:
  11.7 59.9 %all-gather.6.cloned.1.call-done = bf16[512,1024]{1,0:T(8,128)(2,1)} async-done(((bf16[16,1024]{1,0:T(8,128)(2,1)}), bf16[512,1024]{1,0:T(8,128)(2,1)}) %all-gather.6.cloned.1.call-update) | async-done | bytes 1048592 | tf_op jit(solution)/shard_map/all_gather | solution.py:14
  73.2 58.1 %all-gather.8.cloned.1.call-done = bf16[512,1024]{1,0:T(8,128)(2,1)} async-done(((bf16[16,1024]{1,0:T(8,128)(2,1)}), bf16[512,1024]{1,0:T(8,128)(2,1)}) %all-gather.8.cloned.1.call-update) | async-done | bytes 1048592 | tf_op jit(solution)/shard_map/all_gather | solution.py:15
  131.3 2.3 copy.66
  135.6 59.4 %all-gather.4.cloned.1.call-done = bf16[4096,512]{1,0:T(8,128)(2,1)} async-done(((bf16[128,512]{1,0:T(8,128)(2,1)}), bf16[4096,512]{1,0:T(8,128)(2,1)}) %all-gather.4.cloned.1.call-update) | async-done | bytes 4194320 | tf_op jit(solution)/shard_map/all_gather | solution.py:13
  195.0 7.9 broadcast_in_dim.33
  202.9 3.7 while.50
  202.9 2.8 conditional.9
  202.9 2.8 fusion.20
  206.6 6.8 reduce_max.9
  213.3 17.5 %copy.69 = f32[1024,4096]{1,0:T(8,128)} copy(f32[1024,4096]{0,1:T(8,128)} %get-tuple-element.842) | data formatting | bytes 33554432 | tf_op jit(solution)/shard_map/while | solution.py:89
  230.8 8.0 exponential_reduce_fusion
  240.4 4.1 while.48
  240.4 3.8 conditional.7
  240.4 3.8 convolution_add_fusion
  244.5 3.5 fusion.46
  248.1 4.3 broadcast_in_dim.32
  253.9 8.7 while.49
  253.9 8.3 conditional.8
  256.3 2.5 fusion.9
  258.8 3.5 convolution_add_fusion.1
  262.6 8.9 copy.70
  273.2 227.2 %all-to-all-start = ((bf16[32,1,2]{2,1,0:T(2,128)(2,1)}), bf16[32,1,2]{2,1,0:T(2,128)(2,1)S(1)}, u32[]{:S(2)}, u32[]{:S(2)}) async-start(bf16[32,1,2]{2,1,0:T(2,128)(2,1)} %all_to_all.28), calls=%async_computation.4 | async-start | bytes 32768 | tf_op jit(solution)/shard_map/all_to_all | solution.py:188
  501.3 6.7 all-to-all-done
  508.0 4.0 all-to-all-start.2
  513.1 9.4 all-to-all-done.2
  522.5 3.9 all-to-all-start.1
  526.4 56.0 %all_gather.19 = bf16[32,2,7168]{2,1,0:T(2,128)(2,1)} all-gather(bf16[32,2,896]{2,1,0:T(2,128)(2,1)S(1)} %all-to-all-done.2), channel_id=1, replica_groups=mesh['ctx'=32,'exp'=8] {'exp'}, dimensions={2}, use_global_device_ids=true | all-gather | bytes 1032192 | tf_op jit(solution)/shard_map/all_gather | solution.py:193
  582.5 2.5 reshape.131
  585.0 57.8 %all_gather.18 = bf16[32,2,7168]{2,1,0:T(2,128)(2,1)} all-gather(bf16[32,2,896]{2,1,0:T(2,128)(2,1)S(1)} %all-to-all-done.1), channel_id=1, replica_groups=mesh['ctx'=32,'exp'=8] {'exp'}, dimensions={2}, use_global_device_ids=true | all-gather | bytes 1032192 | tf_op jit(solution)/shard_map/all_gather | solution.py:194
  642.8 3.2 reshape.129
  650.0 2.0 convolution_add_fusion.3
  652.0 3.3 reshape.132
  655.2 56.2 %all_to_all.34 = f32[32,2,7168]{2,1,0:T(2,128)} all-to-all(f32[32,2,7168]{2,1,0:T(2,128)} %reshape.132), channel_id=1, replica_groups=mesh['ctx'=32,'exp'=8] {'ctx'}, dimensions={0} | all-to-all | bytes 3670016 | tf_op jit(solution)/shard_map/all_to_all | solution.py:234
  711.4 3.4 reshape.133
  714.9 6.4 fusion.48
  725.8 2.9 copy.72
  728.8 3.0 fusion.50
  731.8 2.9 copy.74
  734.8 50.4 %psum.7 = f32[32,1,2]{2,0,1:T(8,128)} all-reduce(f32[32,1,2]{2,0,1:T(8,128)S(1)} %all_to_all.26), channel_id=1, replica_groups=mesh['ctx'=32,'exp'=8] {'exp'}, use_global_device_ids=true, to_apply=%region_22.23 | all-reduce | flops 64 | bytes 512 | tf_op jit(solution)/shard_map/psum | solution.py:210
  785.3 7.4 all-to-all-start.4
  792.7 1.9 fusion.24
  794.6 2.0 fusion.26
  796.6 1.9 fusion.25
  802.4 2.0 convolution_convert_fusion.5
  805.2 35.7 %reduce-scatter.14.cloned.1.call-done = f32[128,896]{1,0:T(8,128)} async-done(((f32[128,7168]{1,0:T(8,128)}), f32[128,896]{1,0:T(8,128)}) %reduce-scatter.14.cloned.1.call-update) | async-done | bytes 458768 | tf_op jit(solution)/shard_map/reduce_scatter | solution.py:246
  842.6 144.0 %reduce-scatter.10.cloned.1.call-done = f32[16,1024]{1,0:T(8,128)} async-done(((f32[512,1024]{1,0:T(8,128)}), f32[16,1024]{1,0:T(8,128)}) %reduce-scatter.10.cloned.1.call-update) | async-done | bytes 65552 | tf_op jit(solution)/shard_map/reduce_scatter | solution.py:147
  986.6 146.2 %reduce-scatter.12.cloned.1.call-done = f32[16,1024]{1,0:T(8,128)} async-done(((f32[512,1024]{1,0:T(8,128)}), f32[16,1024]{1,0:T(8,128)}) %reduce-scatter.12.cloned.1.call-update) | async-done | bytes 65552 | tf_op jit(solution)/shard_map/reduce_scatter | solution.py:148
  1132.8 83.6 %reduce-scatter.8.cloned.1.call-done = f32[128,64]{0,1:T(8,128)} async-done(((f32[128,512]{0,1:T(8,128)}), f32[128,64]{0,1:T(8,128)}) %reduce-scatter.8.cloned.1.call-update) | async-done | bytes 32784 | tf_op jit(solution)/shard_map/reduce_scatter | solution.py:150
  (159 shorter events, 32.5 us)
Async XLA Ops:
  7.2 638.8 %copy-start = (bf16[1,7168,128]{2,1,0:T(8,128)(2,1)S(1)}, bf16[1,7168,128]{2,1,0:T(8,128)(2,1)}, u32[]{:S(2)}) copy-start(bf16[1,7168,128]{2,1,0:T(8,128)(2,1)} %param.35) | copy-start | bytes 5505028
  7.2 64.5 %all-gather.6.cloned.1.call-start = ((), (), s32[]{:S(2)}) async-start(), calls=%async_computation.11 | async-start | bytes 1081344 | tf_op jit(solution)/shard_map/all_gather | solution.py:14
  7.9 123.4 %all-gather.8.cloned.1.call-start = ((), (), s32[]{:S(2)}) async-start(), calls=%async_computation.12 | async-start | bytes 1081344 | tf_op jit(solution)/shard_map/all_gather | solution.py:15
  8.7 186.3 %all-gather.4.cloned.1.call-start = ((), (), s32[]{:S(2)}) async-start(), calls=%async_computation.10 | async-start | bytes 4325376 | tf_op jit(solution)/shard_map/all_gather | solution.py:13
  9.4 787.2 %reduce-scatter.6.cloned.1.call-start = ((), (), s32[]{:S(2)}) async-start(), calls=%async_computation.13 | async-start | bytes 8650752 | tf_op jit(solution)/shard_map/reduce_scatter | solution.py:146
  73.2 61.9 %copy-start.3 = (bf16[512,1024]{0,1:T(8,128)(2,1)}, bf16[512,1024]{0,1:T(8,128)(2,1)S(1)}, u32[]{:S(2)}) copy-start(bf16[512,1024]{0,1:T(8,128)(2,1)S(1)} %copy.63) | copy-start | bytes 3145732
  133.6 1.5 copy-start.7
  253.9 1.9 copy-start.1
  271.6 0.7 copy-start.11
  271.6 0.7 copy-start.12
  271.6 0.7 copy-start.13
  271.6 228.8 %copy-start.9 = (bf16[128,896]{1,0:T(8,128)(2,1)S(1)}, bf16[128,896]{1,0:T(8,128)(2,1)}, u32[]{:S(2)}) copy-start(bf16[128,896]{1,0:T(8,128)(2,1)} %param.30) | copy-start | bytes 688132
  271.6 240.5 %copy-start.10 = (bf16[128,896]{1,0:T(8,128)(2,1)S(1)}, bf16[128,896]{1,0:T(8,128)(2,1)}, u32[]{:S(2)}) copy-start(bf16[128,896]{1,0:T(8,128)(2,1)} %param.31) | copy-start | bytes 688132
  273.2 234.8 %all-to-all-start = ((bf16[32,1,2]{2,1,0:T(2,128)(2,1)}), bf16[32,1,2]{2,1,0:T(2,128)(2,1)S(1)}, u32[]{:S(2)}, u32[]{:S(2)}) async-start(bf16[32,1,2]{2,1,0:T(2,128)(2,1)} %all_to_all.28), calls=%async_computation.4 | async-start | bytes 32768 | tf_op jit(solution)/shard_map/all_to_all | solution.py:188
  508.0 14.5 %all-to-all-start.2 = ((bf16[32,2,896]{2,1,0:T(2,128)(2,1)}), bf16[32,2,896]{2,1,0:T(2,128)(2,1)S(1)}, u32[]{:S(2)}, u32[]{:S(2)}) async-start(bf16[32,2,896]{2,1,0:T(2,128)(2,1)} %reshape.130), calls=%async_computation.6 | async-start | bytes 229376 | tf_op jit(solution)/shard_map/all_to_all | solution.py:174
  522.5 62.4 %all-to-all-start.1 = ((bf16[32,2,896]{2,1,0:T(2,128)(2,1)}), bf16[32,2,896]{2,1,0:T(2,128)(2,1)S(1)}, u32[]{:S(2)}, u32[]{:S(2)}) async-start(bf16[32,2,896]{2,1,0:T(2,128)(2,1)} %reshape.128), calls=%async_computation.5 | async-start | bytes 229376 | tf_op jit(solution)/shard_map/all_to_all | solution.py:181
  526.4 314.5 %reduce-scatter.14.cloned.1.call-start = ((), (), s32[]{:S(2)}) async-start(), calls=%async_computation.17 | async-start | bytes 4128768 | tf_op jit(solution)/shard_map/reduce_scatter | solution.py:246
  646.0 1.5 copy-start.6
  646.0 2.0 copy-start.4
  646.0 2.4 copy-start.8
  721.2 265.4 %reduce-scatter.10.cloned.1.call-start = ((), (), s32[]{:S(2)}) async-start(), calls=%async_computation.15 | async-start | bytes 2162688 | tf_op jit(solution)/shard_map/reduce_scatter | solution.py:147
  723.0 1.0 copy-start.2
  728.7 404.1 %reduce-scatter.12.cloned.1.call-start = ((), (), s32[]{:S(2)}) async-start(), calls=%async_computation.16 | async-start | bytes 2162688 | tf_op jit(solution)/shard_map/reduce_scatter | solution.py:148
  785.3 15.0 %all-to-all-start.4 = ((f32[32,1,2]{2,1,0:T(1,128)}), f32[32,1,2]{2,1,0:T(1,128)S(1)}, u32[]{:S(2)}, u32[]{:S(2)}) async-start(f32[32,1,2]{2,1,0:T(1,128)} %bitcast.24), calls=%async_computation.9 | async-start | bytes 32768 | tf_op jit(solution)/shard_map/all_to_all | solution.py:241
  792.7 423.7 %reduce-scatter.8.cloned.1.call-start = ((), (), s32[]{:S(2)}) async-start(), calls=%async_computation.14 | async-start | bytes 294912 | tf_op jit(solution)/shard_map/reduce_scatter | solution.py:150
  792.7 1.9 copy-start.5
Sparse Core Ops, SparseCore 0:
  9.9 61.7 all-gather.5
  73.5 57.7 all-gather.7
  133.2 61.7 all-gather.3
  271.8 404.4 reduce-scatter.5
  721.4 119.4 reduce-scatter.13
  844.0 142.5 reduce-scatter.9
  989.7 143.0 reduce-scatter.11
  1137.7 78.6 reduce-scatter.7
where the time goes:
time: 1230 us; the launch traced here: 1220 us
  waiting for transfers between devices  607 us (49%)
  starting transfers between devices  243 us (20%)
  blocking collectives  220 us (18%)
  local copies, waits for them, and re-layouts  72.9 us (6%)
  matrix products  41.5 us (3%)
  other arithmetic  22.6 us (2%)
  between operations  14.4 us (1%)
    all_to_all x1, starting transfers between devices, expert_backward(): lax.all_to_all(gate_send.reshape(expert_count, CAP), 'ctx', split_axis=0,...  227 us
    reduce_scatter x1, waiting for transfers between devices, attention_backward(): lax.psum_scatter(value_grads, 'ctx', scatter_dimension=0, tiled=True)  146 us
    reduce_scatter x1, waiting for transfers between devices, attention_backward(): lax.psum_scatter(key_grads, 'ctx', scatter_dimension=0, tiled=True)  144 us
    reduce_scatter x1, waiting for transfers between devices, attention_backward(): lax.psum_scatter(latent_part, 'exp', scatter_dimension=1, tiled=True)  83.6 us
    all_gather x1, waiting for transfers between devices, attention_backward(): lax.all_gather(w_uk, 'ctx', axis=0, tiled=True)  59.9 us
    all_gather x1, waiting for transfers between devices, attention_backward(): lax.all_gather(latents, 'ctx', axis=0, tiled=True)  59.4 us
    all_gather x1, waiting for transfers between devices, attention_backward(): lax.all_gather(w_uv, 'ctx', axis=0, tiled=True)  58.1 us
    all_gather x1, blocking collectives, expert_backward(): lax.all_gather(grads_recv, 'exp', axis=2, tiled=True)  57.8 us
  transfers between devices with their start and end apart: 12, of which 10 were waited for; matrix products, arithmetic and copies ran while one was open for 5% of the time, Pallas kernels for 0%

commit v1 on v0

v1 whole, which is shorter than its diff:
```python
import jax
import jax.numpy as jnp
from jax import lax
from jax.experimental import pallas as pl
from jax.experimental.pallas import tpu as pltpu
from jax.sharding import PartitionSpec as P

MESH = pl.DeviceIdType.MESH
HD = 128
CAP = 2
TOK = 128
NC = 32
F32 = jnp.float32
BF16 = jnp.bfloat16
DMA = pltpu.SemaphoreType.DMA
VMEM = pltpu.VMEM


class Place:
    def __init__(self):
        self.c = c = lax.axis_index("ctx")
        self.e = e = lax.axis_index("exp")
        self.z, self.x, self.core = c // 8, (c // 2) % 4, c % 2
        self.y, self.zh = e // 2, e % 2
        p = c % 8
        self.i = c // 4
        self.r = p + (p // 4) * (7 - 2 * p)

    def ctx(self, z, x, core):
        return (z * 8 + x * 2 + core, self.e)

    def exp(self, y, zh):
        return (self.c, y * 2 + zh)

    def member(self, i):
        return 4 * i + self.r + (i % 2) * (3 - 2 * self.r)


def greet(devices, loops):
    barrier = pltpu.get_barrier_semaphore()
    count = 0
    for steps, device in loops:

        def one(k, carry, device=device):
            pl.semaphore_signal(barrier, inc=1, device_id=device(k), device_id_type=MESH)
            return carry

        lax.fori_loop(0, steps, one, 0)
        count += steps
    for device in devices:
        pl.semaphore_signal(barrier, inc=1, device_id=device, device_id_type=MESH)
    pl.semaphore_wait(barrier, count + len(devices))


def send(src, dst, send_sem, recv_sem, device):
    copy = pltpu.make_async_remote_copy(
        src_ref=src,
        dst_ref=dst,
        send_sem=send_sem,
        recv_sem=recv_sem,
        device_id=device,
        device_id_type=MESH,
    )
    copy.start()
    return copy


def drain(ref, sem):
    pltpu.make_async_copy(ref, ref, sem).wait()


def ring_gather(at, pos, left, right, send_sem, recv_sem):
    other = (pos + 2) % 4
    before, after = (pos + 3) % 4, (pos + 1) % 4

    def first():
        for h in range(2):
            send(at(pos, h), at(pos, h), send_sem.at[h], recv_sem.at[h], right)
            send(at(pos, h), at(pos, h), send_sem.at[2 + h], recv_sem.at[2 + h], left)

    def second():
        drain(at(before, 0), recv_sem.at[0])
        send(at(before, 0), at(before, 0), send_sem.at[4], recv_sem.at[4], right)
        drain(at(after, 1), recv_sem.at[3])
        send(at(after, 1), at(after, 1), send_sem.at[5], recv_sem.at[5], left)

    def last():
        drain(at(before, 1), recv_sem.at[1])
        drain(at(after, 0), recv_sem.at[2])
        drain(at(other, 0), recv_sem.at[4])
        drain(at(other, 1), recv_sem.at[5])
        for k in range(6):
            drain(at(pos, 0), send_sem.at[k])

    return first, second, last


def ring_scatter(at, pos, left, right, held, send_sem, recv_sem, add):
    other = (pos + 2) % 4
    before, after = (pos + 3) % 4, (pos + 1) % 4

    def first():
        send(at(other, 0), held.at[0], send_sem.at[0], recv_sem.at[0], right)
        send(at(other, 1), held.at[1], send_sem.at[1], recv_sem.at[1], left)
        send(at(after, 1), held.at[3], send_sem.at[2], recv_sem.at[3], right)
        send(at(before, 0), held.at[4], send_sem.at[3], recv_sem.at[4], left)

    def second():
        drain(held.at[0], recv_sem.at[0])
        add(at(after, 0), held.at[0])
        send(at(after, 0), held.at[2], send_sem.at[4], recv_sem.at[2], right)
        drain(held.at[1], recv_sem.at[1])
        add(at(before, 1), held.at[1])
        send(at(before, 1), held.at[5], send_sem.at[5], recv_sem.at[5], left)

    def last():
        for k in range(2, 6):
            drain(held.at[k], recv_sem.at[k])
        for k in range(6):
            drain(held.at[k], send_sem.at[k])

    return first, second, last


def add_into(dst, src):
    def one(k, carry):
        dst[k] = (dst[k].astype(F32) + src[k].astype(F32)).astype(dst.dtype)
        return carry

    lax.fori_loop(0, dst.shape[0], one, 0)


def gather_kernel(
    q_ref, g_ref, wk_ref, wv_ref, lat_ref, moe_ref,
    qo, go, wko, wvo, lato, rowo,
    own_sem, send_sem, recv_sem, z_send, z_recv, x_send, x_recv, y_send, y_recv,
):
    at = Place()
    c, e = at.c, at.e
    left_x, right_x = at.ctx(at.z, (at.x + 3) % 4, at.core), at.ctx(at.z, (at.x + 1) % 4, at.core)
    left_y, right_y = at.exp((at.y + 3) % 4, at.zh), at.exp((at.y + 1) % 4, at.zh)
    twin, sibling = at.exp(at.y, 1 - at.zh), at.ctx(at.z, at.x, 1 - at.core)
    greet((left_y, right_y, twin), ((NC - 1, lambda k: ((c + 1 + k) % NC, e)),))

    def lanes(h):
        return pl.ds(pl.multiple_of(h * HD, HD), HD)

    rows16 = pl.ds(pl.multiple_of(c * 16, 16), 16)
    own = [
        pltpu.make_async_copy(moe_ref.at[c], rowo.at[e, c], own_sem.at[0]),
        pltpu.make_async_copy(lat_ref, lato.at[at.z, at.x, at.core], own_sem.at[1]),
        pltpu.make_async_copy(q_ref.at[:, lanes(at.i)], qo.at[at.i], own_sem.at[2]),
        pltpu.make_async_copy(g_ref.at[:, lanes(at.i)], go.at[at.i], own_sem.at[3]),
        pltpu.make_async_copy(wk_ref.at[:, lanes(at.i)], wko.at[rows16], own_sem.at[4]),
        pltpu.make_async_copy(wv_ref.at[:, lanes(at.i)], wvo.at[rows16], own_sem.at[5]),
    ]
    for copy in own:
        copy.start()

    def send_rows(k, carry):
        d = (c + 1 + k) % NC
        send(moe_ref.at[d], rowo.at[e, c], send_sem.at[0], recv_sem.at[0], (d, e))
        return carry

    lax.fori_loop(0, NC - 1, send_rows, 0)

    for k in range(1, 4):
        z = (at.z + k) % 4
        send(
            lat_ref, lato.at[at.z, at.x, at.core], z_send.at[k - 1], z_recv.at[k - 1],
            at.ctx(z, at.x, at.core),
        )

    def send_heads(k, carry):
        i = (at.i + 1 + k) % 8
        d = (at.member(i), e)
        send(q_ref.at[:, lanes(i)], qo.at[at.i], send_sem.at[1], recv_sem.at[1], d)
        send(g_ref.at[:, lanes(i)], go.at[at.i], send_sem.at[2], recv_sem.at[2], d)
        return carry

    lax.fori_loop(0, 7, send_heads, 0)

    def send_weights(k, carry):
        d = (c + 1 + k) % NC
        send(wk_ref.at[:, lanes(d // 4)], wko.at[rows16], send_sem.at[3], recv_sem.at[3], (d, e))
        send(wv_ref.at[:, lanes(d // 4)], wvo.at[rows16], send_sem.at[4], recv_sem.at[4], (d, e))
        return carry

    lax.fori_loop(0, NC - 1, send_weights, 0)

    own[0].wait()
    drain(rowo.at[e, pl.ds(0, NC - 1)], recv_sem.at[0])
    twin_copy = send(rowo.at[e], rowo.at[e], z_send.at[3], z_recv.at[3], twin)

    own[1].wait()
    for k in range(1, 4):
        drain(lat_ref, z_recv.at[k - 1])
    x_ring = ring_gather(
        lambda q, h: lato.at[pl.ds(2 * h, 2), q, at.core], at.x, left_x, right_x, x_send, x_recv
    )
    x_ring[0]()
    twin_copy.wait_recv()
    y_ring = ring_gather(
        lambda q, h: rowo.at[2 * q + h], at.y, left_y, right_y, y_send, y_recv
    )
    y_ring[0]()
    x_ring[1]()
    y_ring[1]()
    x_ring[2]()
    core_copy = send(
        lato.at[:, :, at.core], lato.at[:, :, at.core], z_send.at[4], z_recv.at[4], sibling
    )
    y_ring[2]()
    for copy in own[2:]:
        copy.wait()
    drain(rowo.at[e, pl.ds(0, NC - 1)], send_sem.at[0])
    for k, ref in ((1, qo), (2, go)):
        drain(ref.at[pl.ds(0, 7)], send_sem.at[k])
        drain(ref.at[pl.ds(0, 7)], recv_sem.at[k])
    for k, ref in ((3, wko), (4, wvo)):
        drain(ref.at[pl.ds(0, 16 * (NC - 1))], send_sem.at[k])
        drain(ref.at[pl.ds(0, 16 * (NC - 1))], recv_sem.at[k])
    for k in range(3):
        drain(lat_ref, z_send.at[k])
    twin_copy.wait_send()
    core_copy.wait()


def gather_inputs(queries, grad_heads, w_uk, w_uv, latents, messages):
    anywhere = pl.BlockSpec(memory_space=pl.ANY)
    depth = messages.shape[1]
    return pl.pallas_call(
        gather_kernel,
        out_shape=(
            jax.ShapeDtypeStruct((8, TOK, HD), BF16),
            jax.ShapeDtypeStruct((8, TOK, HD), BF16),
            jax.ShapeDtypeStruct((16 * NC, HD), BF16),
            jax.ShapeDtypeStruct((16 * NC, HD), BF16),
            jax.ShapeDtypeStruct((4, 4, 2, TOK, 512), BF16),
            jax.ShapeDtypeStruct((8, NC, depth, 128), BF16),
        ),
        in_specs=[anywhere] * 6,
        out_specs=(anywhere,) * 6,
        scratch_shapes=[
            DMA((6,)), DMA((5,)), DMA((5,)), DMA((5,)), DMA((5,)),
            DMA((6,)), DMA((6,)), DMA((6,)), DMA((6,)),
        ],
        compiler_params=pltpu.CompilerParams(collective_id=0, has_side_effects=True),
    )(queries, grad_heads, w_uk, w_uv, latents, messages)


def attention_kernel(
    q_ref, g_ref, wk_ref, wv_ref, lat_ref,
    dq_ref, kg_ref, vg_ref, dl_ref,
    lat_t, probs, dprob, low, tops, o_t, dq_t, dlat,
):
    r = Place().r
    scale = HD**-0.5
    width = 512
    contract_last = (((1,), (1,)), ((), ()))
    contract_first = (((0,), (0,)), ((), ()))

    def tile(t):
        return pl.ds(pl.multiple_of(t * width, width), width)

    def prepare(t, carry):
        lat_t[:, tile(t)] = lat_ref[tile(t), :].T
        dlat[tile(t), :] = jnp.zeros((width, 512), F32)
        return carry

    lax.fori_loop(0, 8, prepare, 0)
    kg_ref[...] = jnp.zeros_like(kg_ref)
    vg_ref[...] = jnp.zeros_like(vg_ref)
    column = lax.broadcasted_iota(jnp.int32, (1, 256), 1)
    key_at = lax.broadcasted_iota(jnp.int32, (width, 1), 0)

    def chunk(j, carry):
        rows = pl.ds(pl.multiple_of(j * 256, 256), 256)
        q, g = q_ref[rows, :], g_ref[rows, :]
        q_lat = lax.dot_general(q, wk_ref[...], contract_last, preferred_element_type=F32).astype(BF16)
        g_lat = lax.dot_general(g, wv_ref[...], contract_last, preferred_element_type=F32).astype(BF16)
        first_block = 8 * j + r
        second_block = 8 * j + 7 - r
        position = column + jnp.where(column < TOK, first_block * TOK, (second_block - 1) * TOK)
        o_t[...] = jnp.zeros_like(o_t)
        dq_t[...] = jnp.zeros_like(dq_t)

        def score(t, state):
            top, total = state
            keys = lat_ref[tile(t), :]
            s = lax.dot_general(keys, q_lat, contract_last, preferred_element_type=F32) * scale
            s = jnp.where(key_at + t * width <= position, s, -jnp.inf)
            new_top = jnp.maximum(top, jnp.max(s, axis=0, keepdims=True))
            weight = jnp.exp(s - new_top)
            probs[tile(t), :] = weight
            tops[t] = jnp.broadcast_to(new_top, (8, 256))
            dprob[tile(t), :] = lax.dot_general(keys, g_lat, contract_last, preferred_element_type=F32)
            total = total * jnp.exp(top - new_top) + jnp.sum(weight, axis=0, keepdims=True)
            return new_top, total

        top, total = lax.fori_loop(
            0, 2 * (j + 1), score, (jnp.full((1, 256), -1e30, F32), jnp.zeros((1, 256), F32))
        )
        inverse = 1.0 / total

        def output(t, delta):
            factor = jnp.exp(tops[t][0:1, :] - top) * inverse
            prob = probs[tile(t), :] * factor
            prob_low = prob.astype(BF16)
            probs[tile(t), :] = prob
            low[tile(t), :] = prob_low
            o_t[...] += jnp.dot(lat_t[:, tile(t)], prob_low, preferred_element_type=F32)
            return delta + jnp.sum(prob_low.astype(F32) * dprob[tile(t), :], axis=0, keepdims=True)

        delta = lax.fori_loop(0, 2 * (j + 1), output, jnp.zeros((1, 256), F32))

        def gradient(t, carry):
            dscore = (probs[tile(t), :] * (dprob[tile(t), :] - delta) * scale).astype(BF16)
            dq_t[...] += jnp.dot(lat_t[:, tile(t)], dscore, preferred_element_type=F32)
            dlat[tile(t), :] += jnp.dot(dscore, q_lat, preferred_element_type=F32) + jnp.dot(
                low[tile(t), :], g_lat, preferred_element_type=F32
            )
            return carry

        lax.fori_loop(0, 2 * (j + 1), gradient, 0)
        dq_low = dq_t[...].astype(BF16)
        dq_ref[rows, :] = lax.dot_general(
            dq_low, wk_ref[...], contract_first, preferred_element_type=F32
        ).astype(BF16)
        kg_ref[...] += jnp.dot(dq_low, q, preferred_element_type=F32)
        vg_ref[...] += jnp.dot(o_t[...].astype(BF16), g, preferred_element_type=F32)
        return carry

    lax.fori_loop(0, 4, chunk, 0)

    def finish(t, carry):
        dl_ref[tile(t), :] = dlat[tile(t), :].astype(BF16)
        return carry

    lax.fori_loop(0, 8, finish, 0)


def attention(q, g, wk, wv, lat):
    whole = pl.BlockSpec(memory_space=VMEM)
    return pl.pallas_call(
        attention_kernel,
        out_shape=(
            jax.ShapeDtypeStruct((1024, HD), BF16),
            jax.ShapeDtypeStruct((512, HD), F32),
            jax.ShapeDtypeStruct((512, HD), F32),
            jax.ShapeDtypeStruct((4096, 512), BF16),
        ),
        in_specs=[whole] * 5,
        out_specs=(whole,) * 4,
        scratch_shapes=[
            VMEM((512, 4096), BF16),
            VMEM((4096, 256), F32),
            VMEM((4096, 256), F32),
            VMEM((4096, 256), BF16),
            VMEM((8, 8, 256), F32),
            VMEM((512, 256), F32),
            VMEM((512, 256), F32),
            VMEM((4096, 512), F32),
        ],
        compiler_params=pltpu.CompilerParams(vmem_limit_bytes=56 * 1024 * 1024),
    )(q, g, wk, wv, lat)


def scatter_kernel(
    dl_ref, dq_ref, kg_ref, vg_ref, mb_ref,
    dqo, dlo, kgo, vgo, mo,
    part, core_held, x_held, y_part, y_held, z_part, z_held, m_part, m_held, twin_part, twin_held,
    m_send, kv_held,
    own_sem, send_sem, recv_sem, x_send, x_recv, y_send, y_recv, my_send, my_recv, z_send, z_recv,
):
    at = Place()
    c, e = at.c, at.e
    left_x, right_x = at.ctx(at.z, (at.x + 3) % 4, at.core), at.ctx(at.z, (at.x + 1) % 4, at.core)
    left_y, right_y = at.exp((at.y + 3) % 4, at.zh), at.exp((at.y + 1) % 4, at.zh)
    twin, sibling = at.exp(at.y, 1 - at.zh), at.ctx(at.z, at.x, 1 - at.core)

    def along_z(k):
        place = (at.zh * 4 + at.z + k) % 8
        return place // 4, place % 4, ((place % 4) * 8 + c % 8, at.y * 2 + place // 4)

    far = [
        (((at.z + k) % 4) * 8 + c % 8, at.y * 2 + 1 - at.zh) for k in range(1, 4)
    ]
    greet((left_y, right_y, twin, *far), ((NC - 1, lambda k: ((c + 1 + k) % NC, e)),))

    def lanes(h):
        return pl.ds(pl.multiple_of(h * HD, HD), HD)

    def rows16(d):
        return pl.ds(pl.multiple_of(d * 16, 16), 16)

    core_copy = send(dl_ref.at[:, :, 1 - at.core], core_held, send_sem.at[0], recv_sem.at[0], sibling)
    own = [
        pltpu.make_async_copy(dl_ref.at[:, :, at.core], part, own_sem.at[0]),
        pltpu.make_async_copy(mb_ref, m_part, own_sem.at[1]),
        pltpu.make_async_copy(dq_ref.at[at.i], dqo.at[:, lanes(at.i)], own_sem.at[2]),
        pltpu.make_async_copy(kg_ref.at[rows16(c)], kv_held.at[0, c], own_sem.at[3]),
        pltpu.make_async_copy(vg_ref.at[rows16(c)], kv_held.at[1, c], own_sem.at[4]),
    ]
    for copy in own:
        copy.start()
    own[1].wait()
    my_ring = ring_scatter(
        lambda q, h: m_part.at[2 * q + h], at.y, left_y, right_y, m_held, my_send, my_recv, add_into
    )
    my_ring[0]()

    def send_heads(k, carry):
        i = (at.i + 1 + k) % 8
        send(dq_ref.at[i], dqo.at[:, lanes(at.i)], send_sem.at[1], recv_sem.at[1], (at.member(i), e))
        return carry

    lax.fori_loop(0, 7, send_heads, 0)

    def send_weights(k, carry):
        d = (c + 1 + k) % NC
        send(kg_ref.at[rows16(d)], kv_held.at[0, c], send_sem.at[2], recv_sem.at[2], (d, e))
        send(vg_ref.at[rows16(d)], kv_held.at[1, c], send_sem.at[3], recv_sem.at[3], (d, e))
        return carry

    lax.fori_loop(0, NC - 1, send_weights, 0)

    own[0].wait()
    core_copy.wait_recv()

    def add_core(k, carry):
        add_into(part.at[k], core_held.at[k])
        return carry

    lax.fori_loop(0, 4, add_core, 0)
    x_ring = ring_scatter(
        lambda q, h: part.at[pl.ds(2 * h, 2), q], at.x, left_x, right_x, x_held, x_send, x_recv, add_into
    )
    x_ring[0]()
    my_ring[1]()
    x_ring[1]()
    my_ring[2]()

    def twin_out(k, carry):
        h = 1 - at.zh
        twin_part[k] = (
            m_part[2 * at.y + h, k].astype(F32) + m_held[2 + h, k].astype(F32) + m_held[4 + h, k].astype(F32)
        ).astype(BF16)
        return carry

    lax.fori_loop(0, NC, twin_out, 0)
    twin_copy = send(twin_part, twin_held, send_sem.at[4], recv_sem.at[4], twin)
    x_ring[2]()

    def x_sum(z, carry):
        total = part[z, at.x].astype(F32) + x_held[2 + z // 2, z % 2].astype(F32) + x_held[4 + z // 2, z % 2].astype(F32)
        low = total.astype(BF16)
        for q in range(4):
            y_part[q, z] = low[:, q * 128 : (q + 1) * 128]
        return carry

    lax.fori_loop(0, 4, x_sum, 0)
    y_ring = ring_scatter(
        lambda q, h: y_part.at[q, pl.ds(2 * h, 2)], at.y, left_y, right_y, y_held, y_send, y_recv, add_into
    )
    y_ring[0]()
    twin_copy.wait_recv()

    def twin_sum(k, carry):
        h = at.zh
        m_send[k] = (
            m_part[2 * at.y + h, k].astype(F32) + m_held[2 + h, k].astype(F32) + m_held[4 + h, k].astype(F32)
            + twin_held[k].astype(F32)
        )
        return carry

    lax.fori_loop(0, NC, twin_sum, 0)
    own_rows = pltpu.make_async_copy(m_send.at[c], mo.at[c], own_sem.at[5])
    own_rows.start()

    def send_rows(k, carry):
        d = (c + 1 + k) % NC
        send(m_send.at[d], mo.at[c], send_sem.at[5], recv_sem.at[5], (d, e))
        return carry

    lax.fori_loop(0, NC - 1, send_rows, 0)
    y_ring[1]()
    y_ring[2]()

    def y_sum(z, carry):
        z_part[z] = (
            y_part[at.y, z].astype(F32) + y_held[2 + z // 2, z % 2].astype(F32) + y_held[4 + z // 2, z % 2].astype(F32)
        )
        return carry

    lax.fori_loop(0, 4, y_sum, 0)
    for k in range(1, 8):
        _, z, device = along_z(k)
        send(z_part.at[z], z_held.at[k - 1], z_send.at[k - 1], z_recv.at[k - 1], device)

    own[3].wait()
    own[4].wait()
    drain(kv_held.at[0, pl.ds(0, NC - 1)], recv_sem.at[2])
    drain(kv_held.at[1, pl.ds(0, NC - 1)], recv_sem.at[3])
    for n, out in ((0, kgo), (1, vgo)):
        for h in range(8):
            out[:, h * HD : (h + 1) * HD] = (kv_held[n, 4 * h] + kv_held[n, 4 * h + 1]) + (
                kv_held[n, 4 * h + 2] + kv_held[n, 4 * h + 3]
            )
    for k in range(7):
        drain(z_held.at[k], z_recv.at[k])
    total = z_part[at.z]
    for k in range(7):
        total = total + z_held[k]
    dlo[...] = total

    for k in range(7):
        drain(z_held.at[k], z_send.at[k])
    own[2].wait()
    own_rows.wait()
    core_copy.wait_send()
    twin_copy.wait_send()
    drain(dq_ref.at[pl.ds(0, 7)], send_sem.at[1])
    drain(dq_ref.at[pl.ds(0, 7)], recv_sem.at[1])
    drain(kv_held.at[0, pl.ds(0, NC - 1)], send_sem.at[2])
    drain(kv_held.at[1, pl.ds(0, NC - 1)], send_sem.at[3])
    drain(m_send.at[pl.ds(0, NC - 1)], send_sem.at[5])
    drain(m_send.at[pl.ds(0, NC - 1)], recv_sem.at[5])


def scatter_outputs(dl, dq, kg, vg, mb):
    anywhere = pl.BlockSpec(memory_space=pl.ANY)
    whole = pl.BlockSpec(memory_space=VMEM)
    return pl.pallas_call(
        scatter_kernel,
        out_shape=(
            jax.ShapeDtypeStruct((TOK, 8 * HD), BF16),
            jax.ShapeDtypeStruct((TOK, 128), F32),
            jax.ShapeDtypeStruct((16, 8 * HD), F32),
            jax.ShapeDtypeStruct((16, 8 * HD), F32),
            jax.ShapeDtypeStruct((NC, 16, 128), F32),
        ),
        in_specs=[anywhere] * 5,
        out_specs=(anywhere, whole, whole, whole, anywhere),
        scratch_shapes=[
            VMEM((4, 4, TOK, 512), BF16),
            VMEM((4, 4, TOK, 512), BF16),
            VMEM((6, 2, TOK, 512), BF16),
            VMEM((4, 4, TOK, 128), BF16),
            VMEM((6, 2, TOK, 128), BF16),
            VMEM((4, TOK, 128), F32),
            VMEM((7, TOK, 128), F32),
            VMEM((8, NC, 16, 128), BF16),
            VMEM((6, NC, 16, 128), BF16),
            VMEM((NC, 16, 128), BF16),
            VMEM((NC, 16, 128), BF16),
            VMEM((NC, 16, 128), F32),
            VMEM((2, NC, 16, HD), F32),
            DMA((6,)), DMA((6,)), DMA((6,)), DMA((6,)), DMA((6,)), DMA((6,)), DMA((6,)),
            DMA((6,)), DMA((6,)), DMA((7,)), DMA((7,)),
        ],
        compiler_params=pltpu.CompilerParams(
            collective_id=1, has_side_effects=True, vmem_limit_bytes=56 * 1024 * 1024
        ),
    )(dl, dq, kg, vg, mb)


def on_device(
    queries, grad_heads, latents, w_uk, w_uv, moe_in, grad_out, routes, slots, gates, w_gate, w_up, w_down
):
    slot_count = NC * CAP
    destination = jnp.where(slots >= 0, routes * CAP + slots, -1)
    matches = (
        destination[:, :, None] == jnp.arange(slot_count, dtype=jnp.int32)[None, None, :]
    ).astype(F32)
    selector = jnp.sum(matches, axis=1)
    selector_low = selector.astype(BF16)
    pick = (((0,), (0,)), ((), ()))
    rows_send = lax.dot_general(selector_low, moe_in, pick, preferred_element_type=F32).astype(BF16)
    grads_send = lax.dot_general(selector_low, grad_out, pick, preferred_element_type=F32).astype(BF16)
    gate_send = jnp.sum(matches * gates.astype(F32)[:, :, None], axis=(0, 1)).astype(BF16)
    messages = jnp.concatenate(
        [
            rows_send.reshape(NC, 14, 128),
            grads_send.reshape(NC, 14, 128),
            jnp.broadcast_to(gate_send.reshape(NC, CAP, 1), (NC, CAP, 128)),
            jnp.zeros((NC, 2, 128), BF16),
        ],
        axis=1,
    )
    q, g, wk, wv, lat, rows = gather_inputs(queries, grad_heads, w_uk, w_uv, latents, messages)

    rows = rows.reshape(8, NC, 32, 128)

    def full(first):
        part = rows[:, :, first : first + 14].reshape(8, NC, CAP, 7, 128)
        return part.transpose(1, 2, 0, 3, 4).reshape(slot_count, 8 * 896)

    rows_flat, grads_flat = full(0), full(14)
    gate_column = rows[0, :, 28:30, 0].reshape(slot_count, 1).astype(F32)
    gate_weight, up_weight, down_weight = w_gate[0], w_up[0], w_down[0]
    last = (((1,), (1,)), ((), ()))
    hidden_gate = jnp.dot(rows_flat, gate_weight, preferred_element_type=F32)
    hidden_up = jnp.dot(rows_flat, up_weight, preferred_element_type=F32)
    sigmoid_gate = jax.nn.sigmoid(hidden_gate)
    activation = hidden_gate * sigmoid_gate * hidden_up
    act_grad = lax.dot_general(grads_flat, down_weight, last, preferred_element_type=F32)
    gate_part = jnp.sum(act_grad * activation, axis=1)
    scaled_grad = gate_column * act_grad
    scaled_act = (gate_column * activation).astype(BF16)
    down_grad = lax.dot_general(scaled_act, grads_flat, pick, preferred_element_type=F32).astype(BF16)
    grad_gate_in = (
        scaled_grad * hidden_up * sigmoid_gate * (1.0 + hidden_gate * (1.0 - sigmoid_gate))
    ).astype(BF16)
    grad_up_in = (scaled_grad * hidden_gate * sigmoid_gate).astype(BF16)
    gate_wgrad = lax.dot_general(rows_flat, grad_gate_in, pick, preferred_element_type=F32).astype(BF16)
    up_wgrad = lax.dot_general(rows_flat, grad_up_in, pick, preferred_element_type=F32).astype(BF16)
    row_grads = lax.dot_general(grad_gate_in, gate_weight, last, preferred_element_type=F32)
    row_grads = row_grads + lax.dot_general(grad_up_in, up_weight, last, preferred_element_type=F32)
    back = row_grads.astype(BF16).reshape(NC, CAP, 8, 7, 128).transpose(2, 0, 1, 3, 4).reshape(8, NC, 14, 128)
    gate_back = jnp.broadcast_to(gate_part.astype(BF16).reshape(1, NC, CAP, 1), (8, NC, CAP, 128))
    back = jnp.concatenate([back, gate_back], axis=2)

    dq, kg, vg, dl = attention(
        q.reshape(1024, HD), g.reshape(1024, HD), wk, wv, lat.reshape(4096, 512)
    )
    d_queries, d_latents, key_summed, value_summed, returned = scatter_outputs(
        dl.reshape(4, 4, 2, TOK, 512), dq.reshape(8, TOK, HD), kg, vg, back
    )
    d_latents = lax.dynamic_slice_in_dim(d_latents, (lax.axis_index("exp") % 2) * 64, 64, 1)
    moe_grad = jnp.dot(
        selector, returned[:, :14].reshape(slot_count, 896), precision=lax.Precision.HIGHEST
    ).astype(BF16)
    gate_grads = jnp.sum(matches * returned[:, 14:16, 0].reshape(1, 1, slot_count), axis=2)
    return (
        d_queries, d_latents, key_summed, value_summed, moe_grad, gate_grads,
        gate_wgrad[None], up_wgrad[None], down_grad[None],
    )


def solution(mesh):
    rows = P("ctx", "exp")
    in_specs = (
        rows, rows, P("ctx", None), rows, rows, rows, rows, P("ctx", None), P("ctx", None), P("ctx", None),
        P("ctx", None, "exp"), P("ctx", None, "exp"), P("ctx", "exp", None),
    )
    out_specs = (
        rows, rows, rows, rows, rows, P("ctx", None),
        P("ctx", None, "exp"), P("ctx", None, "exp"), P("ctx", "exp", None),
    )
    return jax.shard_map(on_device, mesh=mesh, in_specs=in_specs, out_specs=out_specs, check_vma=False)
```

time: 1230 us -> 213 us (0.17)
  waiting for transfers between devices: 607 us -> 0 us
  starting transfers between devices: 243 us -> 0 us
  blocking collectives: 220 us -> 0 us
  Pallas kernels: 0 us -> 167 us
  local copies, waits for them, and re-layouts: 72.9 us -> 22.5 us
  matrix products: 41.5 us -> 16.9 us
  other arithmetic: 22.6 us -> 5.57 us
  between operations: 14.4 us -> 0.87 us
    reduce_scatter x5 -> x0, waiting for transfers between devices: 409 us -> none  [the longest x1 146 us: attention_backward(): lax.psum_scatter(value_grads, 'ctx', scatter_dimension=0, tiled=True)]
    all_to_all x4 -> x0, starting transfers between devices: 242 us -> none  [the longest x1 227 us: expert_backward(): lax.all_to_all(gate_send.reshape(expert_count, CAP), 'ctx', split_axis=0,...]
    all_gather x3 -> x0, waiting for transfers between devices: 177 us -> none  [the longest x1 59.9 us: attention_backward(): lax.all_gather(w_uk, 'ctx', axis=0, tiled=True)]
    pallas_call x0 -> x3, Pallas kernels: none -> 167 us  [the longest x1 70.7 us: gather_inputs(): pl.pallas_call(gather_kernel, out_shape=(jax.ShapeDtypeStruct((8, TOK, HD...]
    all_gather x2 -> x0, blocking collectives: 114 us -> none  [the longest x1 57.8 us: expert_backward(): lax.all_gather(grads_recv, 'exp', axis=2, tiled=True)]
    all_to_all x1 -> x0, blocking collectives: 56.2 us -> none  [expert_backward(): lax.all_to_all(row_grads.reshape(expert_count, CAP, model_width), 'ctx',...]
    psum x1 -> x0, blocking collectives: 50.4 us -> none  [expert_backward(): gate_summed = lax.psum(jnp.sum(act_grad * activation, axis=1), 'exp')]
    while x2 -> x0, local copies, waits for them, and re-layouts: 26.4 us -> none  [the longest x1 17.5 us: attention_backward(): lax.fori_loop(0, block_count, output_step, jnp.zeros((row_count, latent_w...]
  transfers between devices with their start and end apart: 12 -> 0, of which waited for: 10 -> 0; matrix products, arithmetic and copies ran while one was open for 5% -> 0% of each run, Pallas kernels for 0% -> 0%
where the time goes in v1:
time: 213 us
  Pallas kernels  167 us (78%)
  local copies, waits for them, and re-layouts  22.5 us (11%)
  matrix products  16.9 us (8%)
  other arithmetic  5.57 us (3%)
    pallas_call x1, Pallas kernels, gather_inputs(): pl.pallas_call(gather_kernel, out_shape=(jax.ShapeDtypeStruct((8, TOK, HD...  70.7 us
    pallas_call x1, Pallas kernels, scatter_outputs(): pl.pallas_call(scatter_kernel, out_shape=(jax.ShapeDtypeStruct((TOK, 8 *...  55.4 us
    pallas_call x1, Pallas kernels, attention(): pl.pallas_call(attention_kernel, out_shape=(jax.ShapeDtypeStruct((1024, H...  40.7 us
    reshape x2, local copies, waits for them, and re-layouts, full(): return part.transpose(1, 2, 0, 3, 4).reshape(slot_count, 8 * 896)  5.02 us

profile of v1, /device:TPU:8, one launch (start us, length us, event | category | flops | bytes accessed | tf_op | source)
XLA Modules:
  0.0 212.7 jit_solution(6799079749111490506)
XLA Ops:
  0.7 0.8 add_select_fusion
  1.5 0.7 convert_element_type.74
  2.2 0.1 convert_reduce_fusion
  2.3 0.1 convert_element_type.76
  2.4 0.1 broadcast_in_dim.30
  2.6 1.1 convolution_convert_fusion.4
  3.7 0.1 reshape.87
  3.8 1.1 convolution_convert_fusion.5
  4.9 0.1 reshape.86
  5.1 0.1 pad.5.clone
  5.2 0.8 maximum_maximum_fusion.moe_ref
  6.0 70.7 %shard_map.196 = (bf16[8,128,128]{2,1,0:T(8,128)(2,1)}, bf16[8,128,128]{2,1,0:T(8,128)(2,1)}, bf16[512,128]{1,0:T(8,128)(2,1)}, bf16[512,128]{1,0:T(8,128)(2,1)}...) custom-call(bf16[128,1024]{1,0:T(8,128)(2,1)} %q_ref.1, bf16[128,1024]{1,0:T(8,128)(2,1)} %g_ref.1, ...), custom_call_target="tpu_custom_call" | custom-call | tf_op jit(solution)/shard_map/pallas_call | solution.py:232
  76.8 40.7 %shard_map.197 = (bf16[1024,128]{1,0:T(8,128)(2,1)}, f32[512,128]{1,0:T(8,128)}, f32[512,128]{1,0:T(8,128)}, bf16[4096,512]{1,0:T(8,128)(2,1)}) custom-call(bf16[1024,128]{1,0:T(8,128)(2,1)} %bitcast.57, bf16[1024,128]{1,0:T(8,128)(2,1)} %bitcast.58, bf16[512,128]{1,0:T(8,128)(2,1)} %get-tuple-element.26.wk_ref, bf16[512,128]{1,0:T(8,128)(2,1)} %get-tuple-element.27.wv_ref, ...), custom_call_target="tpu_custom_call" | custom-call | tf_op jit(solution)/shard_map/pallas_call | solution.py:345
  117.5 1.4 fusion.16
  119.0 0.2 copy.37
  119.2 1.4 copy.38
  120.6 2.1 %reshape.96 = bf16[64,7168]{1,0:T(8,128)(2,1)S(1)} reshape(bf16[32,2,8,7,128]{4,3,2,1,0:T(8,128)(2,1)} %copy.38) | data formatting | bytes 1835008 | tf_op jit(solution)/shard_map/reshape | solution.py:597
  122.8 2.0 fusion.9
  124.8 0.2 copy.35
  125.1 1.4 copy.36
  126.4 2.9 %reshape.94 = bf16[64,7168]{1,0:T(8,128)(2,1)} reshape(bf16[32,2,8,7,128]{4,3,2,1,0:T(8,128)(2,1)} %copy.36) | data formatting | bytes 1835008 | tf_op jit(solution)/shard_map/reshape | solution.py:597
  129.3 2.5 %fusion.11 = f32[64,128]{1,0:T(8,128)S(1)} fusion(bf16[64,7168]{1,0:T(8,128)(2,1)} %reshape.94, bf16[1,128,7168]{2,1,0:T(8,128)(2,1)} %param.25), kind=kOutput, calls=%fused_computation.15 | convolution fusion | flops 117440512 | bytes 2785280 | tf_op jit(solution)/shard_map/dot_general | solution.py:607
  131.9 0.9 convert_reduce_fusion.1
  132.8 0.1 reshape.100
  132.9 0.6 multiply_convert_fusion.2
  133.5 0.1 convert_element_type.83
  133.6 0.1 broadcast_in_dim.32
  133.8 0.7 fusion.4
  134.5 0.7 copy-done.2
  135.3 1.7 fusion.3
  137.0 3.1 %reshape.97 = bf16[32,2,8,7,128]{4,3,2,1,0:T(8,128)(2,1)} reshape(bf16[64,7168]{1,0:T(8,128)(2,1)} %fusion.3) | data formatting | bytes 1835008 | tf_op jit(solution)/shard_map/reshape | solution.py:620
  140.0 1.9 copy.39
  141.9 0.4 copy.40
  142.3 1.4 pad_maximum_fusion.mb_ref
  143.7 55.4 %shard_map.198 = (bf16[128,1024]{1,0:T(8,128)(2,1)}, f32[128,128]{1,0:T(8,128)}, f32[16,1024]{1,0:T(8,128)}, f32[16,1024]{1,0:T(8,128)}, f32[32,16,128]{2,1,0:T(8,128)}) custom-call(bf16[4,4,2,128,512]{4,3,2,1,0:T(8,128)(2,1)} %bitcast.50, bf16[8,128,128]{2,1,0:T(8,128)(2,1)} %bitcast.56, f32[512,128]{1,0:T(8,128)} %get-tuple-element.31.kg_ref, ...), custom_call_target="tpu_custom_call" | custom-call | tf_op jit(solution)/shard_map/pallas_call | solution.py:534
  199.2 0.9 constant_dynamic-slice_fusion
  200.1 0.7 copy.41
  200.8 1.0 reshape.99
  201.8 1.3 convolution_convert_fusion.3
  203.1 1.0 slice_reduce_fusion
  204.1 0.1 mul.84
  204.2 0.7 select_reduce_fusion
  204.9 1.9 fusion
  206.8 1.9 fusion.1
  208.8 2.0 fusion.2
  210.7 0.7 copy.45
  211.5 0.6 copy.46
  212.1 0.6 copy.47
  (16 shorter events, 0.0 us)
Async XLA Ops:
  0.6 132.3 %copy-start = (bf16[1,7168,128]{2,1,0:T(8,128)(2,1)S(1)}, bf16[1,7168,128]{2,1,0:T(8,128)(2,1)}, u32[]{:S(2)}) copy-start(bf16[1,7168,128]{2,1,0:T(8,128)(2,1)} %param.23) | copy-start | bytes 5505028
  76.8 40.8 %copy-start.4 = (bf16[8,32,32,128]{3,2,1,0:T(8,128)(2,1)S(1)}, bf16[8,32,32,128]{3,2,1,0:T(8,128)(2,1)}, u32[]{:S(2)}) copy-start(bf16[8,32,32,128]{3,2,1,0:T(8,128)(2,1)} %get-tuple-element.33) | copy-start | bytes 6291460
  122.7 2.1 copy-start.3
  133.8 1.5 copy-start.2
  206.8 1.9 copy-start.1
  208.8 2.0 copy-start.5
  208.8 2.7 %copy-start.7 = (f32[16,1024]{1,0:T(8,128)S(1)}, f32[16,1024]{1,0:T(8,128)}, u32[]{:S(2)}) copy-start(f32[16,1024]{1,0:T(8,128)} %get-tuple-element.85) | copy-start | bytes 196612
  208.8 3.3 %copy-start.6 = (f32[16,1024]{1,0:T(8,128)S(1)}, f32[16,1024]{1,0:T(8,128)}, u32[]{:S(2)}) copy-start(f32[16,1024]{1,0:T(8,128)} %get-tuple-element.86) | copy-start | bytes 196612

commit v2 on v1

v2 whole, which is shorter than its diff:
```python
import jax
import jax.numpy as jnp
from jax import lax
from jax.experimental import pallas as pl
from jax.experimental.pallas import tpu as pltpu
from jax.sharding import PartitionSpec as P

MESH = pl.DeviceIdType.MESH
HD = 128
CAP = 2
TOK = 128
NC = 32
F32 = jnp.float32
BF16 = jnp.bfloat16
DMA = pltpu.SemaphoreType.DMA
VMEM = pltpu.VMEM


class Place:
    def __init__(self):
        self.c = c = lax.axis_index("ctx")
        self.e = e = lax.axis_index("exp")
        self.z, self.x, self.core = c // 8, (c // 2) % 4, c % 2
        self.y, self.zh = e // 2, e % 2
        p = c % 8
        self.i = c // 4
        self.r = p + (p // 4) * (7 - 2 * p)

    def ctx(self, z, x, core):
        return (z * 8 + x * 2 + core, self.e)

    def exp(self, y, zh):
        return (self.c, y * 2 + zh)

    def member(self, i):
        return 4 * i + self.r + (i % 2) * (3 - 2 * self.r)


def greet(devices, loops):
    barrier = pltpu.get_barrier_semaphore()
    count = 0
    for steps, device in loops:

        def one(k, carry, device=device):
            pl.semaphore_signal(barrier, inc=1, device_id=device(k), device_id_type=MESH)
            return carry

        lax.fori_loop(0, steps, one, 0)
        count += steps
    for device in devices:
        pl.semaphore_signal(barrier, inc=1, device_id=device, device_id_type=MESH)
    pl.semaphore_wait(barrier, count + len(devices))


def send(src, dst, send_sem, recv_sem, device):
    copy = pltpu.make_async_remote_copy(
        src_ref=src,
        dst_ref=dst,
        send_sem=send_sem,
        recv_sem=recv_sem,
        device_id=device,
        device_id_type=MESH,
    )
    copy.start()
    return copy


def drain(ref, sem):
    pltpu.make_async_copy(ref, ref, sem).wait()


def ring_gather(at, pos, left, right, send_sem, recv_sem):
    other = (pos + 2) % 4
    before, after = (pos + 3) % 4, (pos + 1) % 4

    def first():
        for h in range(2):
            send(at(pos, h), at(pos, h), send_sem.at[h], recv_sem.at[h], right)
            send(at(pos, h), at(pos, h), send_sem.at[2 + h], recv_sem.at[2 + h], left)

    def second():
        drain(at(before, 0), recv_sem.at[0])
        send(at(before, 0), at(before, 0), send_sem.at[4], recv_sem.at[4], right)
        drain(at(after, 1), recv_sem.at[3])
        send(at(after, 1), at(after, 1), send_sem.at[5], recv_sem.at[5], left)

    def last():
        drain(at(before, 1), recv_sem.at[1])
        drain(at(after, 0), recv_sem.at[2])
        drain(at(other, 0), recv_sem.at[4])
        drain(at(other, 1), recv_sem.at[5])
        for k in range(6):
            drain(at(pos, 0), send_sem.at[k])

    return first, second, last


def ring_scatter(at, pos, left, right, held, send_sem, recv_sem, add):
    other = (pos + 2) % 4
    before, after = (pos + 3) % 4, (pos + 1) % 4

    def first():
        send(at(other, 0), held.at[0], send_sem.at[0], recv_sem.at[0], right)
        send(at(other, 1), held.at[1], send_sem.at[1], recv_sem.at[1], left)
        send(at(after, 1), held.at[3], send_sem.at[2], recv_sem.at[3], right)
        send(at(before, 0), held.at[4], send_sem.at[3], recv_sem.at[4], left)

    def second():
        drain(held.at[0], recv_sem.at[0])
        add(at(after, 0), held.at[0])
        send(at(after, 0), held.at[2], send_sem.at[4], recv_sem.at[2], right)
        drain(held.at[1], recv_sem.at[1])
        add(at(before, 1), held.at[1])
        send(at(before, 1), held.at[5], send_sem.at[5], recv_sem.at[5], left)

    def last():
        for k in range(2, 6):
            drain(held.at[k], recv_sem.at[k])
        for k in range(6):
            drain(held.at[k], send_sem.at[k])

    return first, second, last


def add_into(dst, src):
    if len(dst.shape) == 2:
        dst[...] = (dst[...].astype(F32) + src[...].astype(F32)).astype(dst.dtype)
        return

    def one(k, carry):
        dst[k] = (dst[k].astype(F32) + src[k].astype(F32)).astype(dst.dtype)
        return carry

    lax.fori_loop(0, dst.shape[0], one, 0)


def fused_kernel(
    q_ref, g_ref, wk_ref, wv_ref, lat_ref, moe_ref, wg_ref, wu_ref, wd_ref,
    dqo, dlo, kgo, vgo, mo, gwgo, gwuo, gwdo,
    lat, lat_t, probs, dprob, tops, o_t, dq_t, dlat, qv, gv, wkv, wvv, dqv, kgv, vgv, kv_held,
    core_out, core_held, part, x_held, y_part, y_held, z_part, z_held,
    rows, spread, xs, ys, wg, wu, wd, gwg, gwu, gwd, dh, m_part, m_held, twin_part, twin_held, m_send,
    own_sem, send_sem, recv_sem, z_send, z_recv, ring_send, ring_recv, core_sem, last_send, last_recv,
):
    at = Place()
    c, e = at.c, at.e
    left_x, right_x = at.ctx(at.z, (at.x + 3) % 4, at.core), at.ctx(at.z, (at.x + 1) % 4, at.core)
    left_y, right_y = at.exp((at.y + 3) % 4, at.zh), at.exp((at.y + 1) % 4, at.zh)
    twin, sibling = at.exp(at.y, 1 - at.zh), at.ctx(at.z, at.x, 1 - at.core)
    far = [(((at.z + k) % 4) * 8 + c % 8, at.y * 2 + 1 - at.zh) for k in range(1, 4)]
    greet((left_y, right_y, twin, *far), ((NC - 1, lambda k: ((c + 1 + k) % NC, e)),))

    def lanes(h):
        return pl.ds(pl.multiple_of(h * HD, HD), HD)

    def rows16(d):
        return pl.ds(pl.multiple_of(d * 16, 16), 16)

    def gather_ring(n, pos, left, right, ref_at):
        return ring_gather(ref_at, pos, left, right, ring_send.at[n], ring_recv.at[n])

    def scatter_ring(n, pos, left, right, ref_at, held):
        return ring_scatter(ref_at, pos, left, right, held, ring_send.at[n], ring_recv.at[n], add_into)

    own = [
        pltpu.make_async_copy(moe_ref.at[c], rows.at[e, c], own_sem.at[0]),
        pltpu.make_async_copy(lat_ref.at[:, lanes(at.y)], lat.at[at.z, at.x, at.core, :, lanes(at.y)], own_sem.at[1]),
        pltpu.make_async_copy(q_ref.at[:, lanes(at.i)], qv.at[at.i], own_sem.at[2]),
        pltpu.make_async_copy(g_ref.at[:, lanes(at.i)], gv.at[at.i], own_sem.at[3]),
        pltpu.make_async_copy(wk_ref.at[:, lanes(at.i)], wkv.at[rows16(c)], own_sem.at[4]),
        pltpu.make_async_copy(wv_ref.at[:, lanes(at.i)], wvv.at[rows16(c)], own_sem.at[5]),
        pltpu.make_async_copy(wg_ref, wg, own_sem.at[6]),
        pltpu.make_async_copy(wu_ref, wu, own_sem.at[7]),
        pltpu.make_async_copy(wd_ref, wd, own_sem.at[8]),
    ]
    for k in (1, 0, 2, 3, 4, 5):
        own[k].start()
    lat_own = lat.at[at.z, at.x, at.core, :, lanes(at.y)]
    for k in range(1, 4):
        send(
            lat_ref.at[:, lanes(at.y)], lat_own, z_send.at[k - 1], z_recv.at[k - 1],
            at.ctx((at.z + k) % 4, at.x, at.core),
        )

    def send_rows(k, carry):
        d = (c + 1 + k) % NC
        send(moe_ref.at[d], rows.at[e, c], send_sem.at[0], recv_sem.at[0], (d, e))
        return carry

    lax.fori_loop(0, NC - 1, send_rows, 0)

    def send_heads(k, carry):
        i = (at.i + 1 + k) % 8
        d = (at.member(i), e)
        send(q_ref.at[:, lanes(i)], qv.at[at.i], send_sem.at[1], recv_sem.at[1], d)
        send(g_ref.at[:, lanes(i)], gv.at[at.i], send_sem.at[2], recv_sem.at[2], d)
        return carry

    lax.fori_loop(0, 7, send_heads, 0)

    def send_weights(k, carry):
        d = (c + 1 + k) % NC
        send(wk_ref.at[:, lanes(d // 4)], wkv.at[rows16(c)], send_sem.at[3], recv_sem.at[3], (d, e))
        send(wv_ref.at[:, lanes(d // 4)], wvv.at[rows16(c)], send_sem.at[4], recv_sem.at[4], (d, e))
        return carry

    lax.fori_loop(0, NC - 1, send_weights, 0)
    for k in (6, 7, 8):
        own[k].start()

    own[1].wait()
    for k in range(3):
        drain(lat_own, z_recv.at[k])
    xa = gather_ring(0, at.x, left_x, right_x, lambda q, h: lat.at[h, q, at.core, :, lanes(at.y)])
    yb = gather_ring(1, at.y, left_y, right_y, lambda q, h: lat.at[2 + h, at.x, at.core, :, lanes(q)])
    ya = gather_ring(2, at.y, left_y, right_y, lambda q, h: lat.at[h, :, at.core, :, lanes(q)])
    xb = gather_ring(3, at.x, left_x, right_x, lambda q, h: lat.at[2 + h, q, at.core])
    xa[0]()
    yb[0]()
    xa[1]()
    yb[1]()
    xa[2]()
    ya[0]()
    yb[2]()
    xb[0]()
    own[0].wait()
    drain(rows.at[e, pl.ds(0, NC - 1)], recv_sem.at[0])
    twin_in = send(rows.at[e], rows.at[e], z_send.at[3], z_recv.at[3], twin)
    ya[1]()
    xb[1]()
    ya[2]()
    core_a = send(lat.at[pl.ds(0, 2), :, at.core], lat.at[pl.ds(0, 2), :, at.core], z_send.at[4], z_recv.at[4], sibling)
    xb[2]()
    core_b = send(lat.at[pl.ds(2, 2), :, at.core], lat.at[pl.ds(2, 2), :, at.core], z_send.at[5], z_recv.at[5], sibling)
    for k in (2, 3, 4, 5):
        own[k].wait()
    for k, ref in ((1, qv), (2, gv)):
        drain(ref.at[pl.ds(0, 7)], recv_sem.at[k])
    for k, ref in ((3, wkv), (4, wvv)):
        drain(ref.at[pl.ds(0, 16 * (NC - 1))], recv_sem.at[k])
    core_a.wait_recv()

    scale = HD**-0.5
    contract_last = (((1,), (1,)), ((), ()))
    contract_first = (((0,), (0,)), ((), ()))
    width = 512

    def tile(t):
        return pl.ds(pl.multiple_of(t * width, width), width)

    def keys_at(t):
        return lat[t // 2, pl.ds(2 * (t % 2), 2)].reshape(width, 512)

    def turn(t, carry):
        lat_t[:, tile(t)] = keys_at(t).T
        return carry

    lax.fori_loop(0, 4, turn, 0)
    core_b.wait_recv()
    lax.fori_loop(4, 8, turn, 0)
    column = lax.broadcasted_iota(jnp.int32, (1, 256), 1)
    key_at = lax.broadcasted_iota(jnp.int32, (width, 1), 0)

    def chunk(j):
        q, g = qv[2 * j : 2 * j + 2].reshape(256, HD), gv[2 * j : 2 * j + 2].reshape(256, HD)
        q_lat = lax.dot_general(q, wkv[...], contract_last, preferred_element_type=F32).astype(BF16)
        g_lat = lax.dot_general(g, wvv[...], contract_last, preferred_element_type=F32).astype(BF16)
        position = column + jnp.where(column < TOK, (8 * j + at.r) * TOK, (8 * j + 6 - at.r) * TOK)
        o_t[...] = jnp.zeros_like(o_t)
        dq_t[...] = jnp.zeros_like(dq_t)

        def score(t, state, masked):
            top, total = state
            keys = keys_at(t)
            s = lax.dot_general(keys, q_lat, contract_last, preferred_element_type=F32) * scale
            if masked:
                s = jnp.where(key_at + t * width <= position, s, -jnp.inf)
            new_top = jnp.maximum(top, jnp.max(s, axis=0, keepdims=True))
            weight = jnp.exp(s - new_top)
            probs[tile(t), :] = weight
            tops[t] = jnp.broadcast_to(new_top, (8, 256))
            dprob[tile(t), :] = lax.dot_general(keys, g_lat, contract_last, preferred_element_type=F32)
            total = total * jnp.exp(top - new_top) + jnp.sum(weight, axis=0, keepdims=True)
            return new_top, total

        state = (jnp.full((1, 256), -1e30, F32), jnp.zeros((1, 256), F32))
        state = lax.fori_loop(0, 2 * j, lambda t, s: score(t, s, False), state)
        top, total = lax.fori_loop(2 * j, 2 * j + 2, lambda t, s: score(t, s, True), state)
        inverse = 1.0 / total

        def output(t, delta):
            prob = probs[tile(t), :] * (jnp.exp(tops[t][0:1, :] - top) * inverse)
            prob_low = prob.astype(BF16)
            probs[tile(t), :] = prob
            o_t[...] += jnp.dot(lat_t[:, tile(t)], prob_low, preferred_element_type=F32)
            return delta + jnp.sum(prob_low.astype(F32) * dprob[tile(t), :], axis=0, keepdims=True)

        delta = lax.fori_loop(0, 2 * j + 2, output, jnp.zeros((1, 256), F32))

        def gradient(t, carry):
            prob = probs[tile(t), :]
            dscore = (prob * (dprob[tile(t), :] - delta) * scale).astype(BF16)
            dq_t[...] += jnp.dot(lat_t[:, tile(t)], dscore, preferred_element_type=F32)
            step = jnp.dot(dscore, q_lat, preferred_element_type=F32) + jnp.dot(
                prob.astype(BF16), g_lat, preferred_element_type=F32
            )
            dlat[tile(t), :] = step if j == 3 else dlat[tile(t), :] + step
            return carry

        lax.fori_loop(0, 2 * j + 2, gradient, 0)
        dq_low = dq_t[...].astype(BF16)
        dq = lax.dot_general(dq_low, wkv[...], contract_first, preferred_element_type=F32).astype(BF16)
        dqv[2 * j : 2 * j + 2] = dq.reshape(2, TOK, HD)
        kg = jnp.dot(dq_low, q, preferred_element_type=F32)
        vg = jnp.dot(o_t[...].astype(BF16), g, preferred_element_type=F32)
        kgv[...] = kg if j == 3 else kgv[...] + kg
        vgv[...] = vg if j == 3 else vgv[...] + vg

    class Reduce:
        def __init__(self, b):
            self.b = b
            self.copy = None
            self.x_ring = scatter_ring(
                4 + b, at.x, left_x, right_x,
                lambda q, h: part.at[b, q, pl.ds(64 * h, 64)], x_held.at[b],
            )
            self.y_ring = scatter_ring(
                8 + b, at.y, left_y, right_y,
                lambda q, h: y_part.at[b, q, pl.ds(64 * h, 64)], y_held.at[b],
            )

        def block(self, x, core):
            return pl.ds(pl.multiple_of((self.b * 8 + x * 2 + core) * TOK, TOK), TOK)

        def to_core(self):
            b = self.b

            def one(x, carry):
                core_out[b, x] = dlat[self.block(x, 1 - at.core), :].astype(BF16)
                return carry

            lax.fori_loop(0, 4, one, 0)
            self.copy = send(core_out.at[b], core_held.at[b], core_sem.at[b], core_sem.at[4 + b], sibling)

        def x1(self):
            b = self.b
            self.copy.wait_recv()

            def one(x, carry):
                part[b, x] = (dlat[self.block(x, at.core), :] + core_held[b, x].astype(F32)).astype(BF16)
                return carry

            lax.fori_loop(0, 4, one, 0)
            self.x_ring[0]()

        def x2(self):
            self.x_ring[1]()

        def x3(self):
            b = self.b
            self.x_ring[2]()
            for h in range(2):
                half = pl.ds(64 * h, 64)
                total = (
                    part[b, at.x, half].astype(F32) + x_held[b, 2 + h].astype(F32) + x_held[b, 4 + h].astype(F32)
                ).astype(BF16)
                for q in range(4):
                    y_part[b, q, half] = total[:, q * 128 : (q + 1) * 128]
            self.y_ring[0]()

        def y2(self):
            self.y_ring[1]()

        def y3(self):
            b = self.b
            self.y_ring[2]()
            for h in range(2):
                half = pl.ds(64 * h, 64)
                z_part[b, half] = (
                    y_part[b, at.y, half].astype(F32) + y_held[b, 2 + h].astype(F32) + y_held[b, 4 + h].astype(F32)
                )

    rs = [Reduce(b) for b in range(4)]

    my = gather_ring(12, at.y, left_y, right_y, lambda q, h: rows.at[2 * q + h])
    mr = scatter_ring(13, at.y, left_y, right_y, lambda q, h: m_part.at[2 * q + h], m_held)

    def slice_lanes(n, f):
        return pl.ds(pl.multiple_of(n * 896 + f * 128, 128), 128)

    def slice_all(n):
        return pl.ds(pl.multiple_of(n * 896, 128), 896)

    def experts():
        for k in (6, 7, 8):
            own[k].wait()

        def unpack(n, carry):
            spread[...] = rows[n].reshape(1024, 128).astype(F32)
            for k in range(2):
                for f in range(7):
                    m = k * 7 + f
                    xs[32 * k : 32 * k + 32, slice_lanes(n, f)] = spread[pl.ds(m, 32, stride=32), :].astype(BF16)
                    ys[32 * k : 32 * k + 32, slice_lanes(n, f)] = spread[pl.ds(14 + m, 32, stride=32), :].astype(BF16)
            return carry

        lax.fori_loop(0, 8, unpack, 0)
        gate = jnp.concatenate([spread[pl.ds(28, 32, stride=32), :], spread[pl.ds(29, 32, stride=32), :]], axis=0)

        def hidden(n, sums):
            a, b, d = sums
            x, dy = xs[:, slice_all(n)], ys[:, slice_all(n)]
            a = a + jnp.dot(x, wg[slice_all(n), :], preferred_element_type=F32)
            b = b + jnp.dot(x, wu[slice_all(n), :], preferred_element_type=F32)
            d = d + lax.dot_general(dy, wd[:, slice_all(n)], contract_last, preferred_element_type=F32)
            return a, b, d

        zero = jnp.zeros((64, 128), F32)
        h1, h2, da = lax.fori_loop(0, 8, hidden, (zero, zero, zero))
        s = 1.0 / (1.0 + jnp.exp(-h1))
        act = h1 * s * h2
        gate_part = jnp.broadcast_to(jnp.sum(da * act, axis=1, keepdims=True), (64, 128))
        scaled = gate * da
        dh[0] = (gate * act).astype(BF16)
        dh[1] = (scaled * h2 * s * (1.0 + h1 * (1.0 - s))).astype(BF16)
        dh[2] = (scaled * h1 * s).astype(BF16)
        for k in range(2):
            spread[pl.ds(14 + k, 32, stride=16), :] = gate_part[32 * k : 32 * k + 32]

        def back(n, carry):
            dx = lax.dot_general(dh[1], wg[slice_all(n), :], contract_last, preferred_element_type=F32)
            dx = dx + lax.dot_general(dh[2], wu[slice_all(n), :], contract_last, preferred_element_type=F32)
            for k in range(2):
                for f in range(7):
                    spread[pl.ds(k * 7 + f, 32, stride=16), :] = dx[32 * k : 32 * k + 32, f * 128 : (f + 1) * 128]
            m_part[n] = spread[0:512, :].reshape(NC, 16, 128).astype(BF16)
            return carry

        lax.fori_loop(0, 8, back, 0)

    def weight_grads(out, k, dst, sem):
        def one(n, carry):
            out[slice_all(n), :] = lax.dot_general(
                xs[:, slice_all(n)], dh[k], contract_first, preferred_element_type=F32
            ).astype(BF16)
            return carry

        lax.fori_loop(0, 8, one, 0)
        copy = pltpu.make_async_copy(out, dst, sem)
        copy.start()
        return copy

    def down_grads():
        def one(n, carry):
            gwd[:, slice_all(n)] = lax.dot_general(
                dh[0], ys[:, slice_all(n)], contract_first, preferred_element_type=F32
            ).astype(BF16)
            return carry

        lax.fori_loop(0, 8, one, 0)
        copy = pltpu.make_async_copy(gwd, gwdo, own_sem.at[11])
        copy.start()
        return copy

    def y_total(h, k):
        return m_part[2 * at.y + h, k].astype(F32) + m_held[2 + h, k].astype(F32) + m_held[4 + h, k].astype(F32)

    def twin_out(k, carry):
        twin_part[k] = y_total(1 - at.zh, k).astype(BF16)
        return carry

    def twin_sum(k, carry):
        m_send[k] = y_total(at.zh, k) + twin_held[k].astype(F32)
        return carry

    def send_back(k, carry):
        d = (c + 1 + k) % NC
        send(m_send.at[d], mo.at[c], send_sem.at[5], recv_sem.at[5], (d, e))
        return carry

    def return_heads(k, carry):
        i = (at.i + 1 + k) % 8
        send(dqv.at[i], dqo.at[:, lanes(at.i)], send_sem.at[6], recv_sem.at[6], (at.member(i), e))
        return carry

    def return_weights(k, carry):
        d = (c + 1 + k) % NC
        send(kgv.at[rows16(d)], kv_held.at[0, c], send_sem.at[7], recv_sem.at[7], (d, e))
        send(vgv.at[rows16(d)], kv_held.at[1, c], send_sem.at[8], recv_sem.at[8], (d, e))
        return carry

    twin_in.wait_recv()
    my[0]()
    chunk(3)
    rs[3].to_core()
    my[1]()
    chunk(2)
    rs[3].x1()
    rs[2].to_core()
    my[2]()
    experts()
    mr[0]()
    chunk(1)
    rs[3].x2()
    rs[2].x1()
    rs[1].to_core()
    mr[1]()
    chunk(0)
    rs[0].to_core()
    lax.fori_loop(0, 7, return_heads, 0)
    lax.fori_loop(0, NC - 1, return_weights, 0)
    kept = [
        pltpu.make_async_copy(dqv.at[at.i], dqo.at[:, lanes(at.i)], own_sem.at[12]),
        pltpu.make_async_copy(kgv.at[rows16(c)], kv_held.at[0, c], own_sem.at[13]),
        pltpu.make_async_copy(vgv.at[rows16(c)], kv_held.at[1, c], own_sem.at[14]),
    ]
    for copy in kept:
        copy.start()
    mr[2]()
    lax.fori_loop(0, NC, twin_out, 0)
    twin_back = send(twin_part, twin_held, z_send.at[6], z_recv.at[6], twin)
    rs[2].x2()
    rs[1].x1()
    rs[3].x3()
    rs[0].x1()
    kept.append(down_grads())
    rs[1].x2()
    rs[3].y2()
    rs[2].x3()
    rs[0].x2()
    twin_back.wait_recv()
    lax.fori_loop(0, NC, twin_sum, 0)
    kept.append(pltpu.make_async_copy(m_send.at[c], mo.at[c], own_sem.at[15]))
    kept[-1].start()
    lax.fori_loop(0, NC - 1, send_back, 0)
    rs[1].x3()
    rs[0].x3()
    rs[3].y3()
    rs[2].y2()
    kept.append(weight_grads(gwg, 1, gwgo, own_sem.at[9]))
    rs[1].y2()
    rs[0].y2()
    kept.append(weight_grads(gwu, 2, gwuo, own_sem.at[10]))
    rs[2].y3()
    rs[1].y3()
    rs[0].y3()
    for k in range(1, 8):
        place = (at.zh * 4 + at.z + k) % 8
        z = place % 4
        device = (z * 8 + c % 8, at.y * 2 + place // 4)
        send(z_part.at[z], z_held.at[k - 1], last_send.at[k - 1], last_recv.at[k - 1], device)

    kept[1].wait()
    kept[2].wait()
    drain(kv_held.at[0, pl.ds(0, NC - 1)], recv_sem.at[7])
    drain(kv_held.at[1, pl.ds(0, NC - 1)], recv_sem.at[8])
    for n, out in ((0, kgo), (1, vgo)):
        for h in range(8):
            out[:, h * HD : (h + 1) * HD] = (kv_held[n, 4 * h] + kv_held[n, 4 * h + 1]) + (
                kv_held[n, 4 * h + 2] + kv_held[n, 4 * h + 3]
            )
    total = z_part[at.z]
    for k in range(7):
        drain(z_held.at[k], last_recv.at[k])
        total = total + z_held[k]
    dlo[...] = total

    kept[0].wait()
    for copy in kept[3:]:
        copy.wait()
    for k in range(7):
        drain(z_held.at[k], last_send.at[k])
    for b in range(4):
        rs[b].copy.wait_send()
    for copy in (twin_in, twin_back, core_a, core_b):
        copy.wait_send()
    for k in range(3):
        drain(lat_own, z_send.at[k])
    drain(rows.at[e, pl.ds(0, NC - 1)], send_sem.at[0])
    for k, ref in ((1, qv), (2, gv)):
        drain(ref.at[pl.ds(0, 7)], send_sem.at[k])
    for k, ref in ((3, wkv), (4, wvv)):
        drain(ref.at[pl.ds(0, 16 * (NC - 1))], send_sem.at[k])
    drain(m_send.at[pl.ds(0, NC - 1)], send_sem.at[5])
    drain(m_send.at[pl.ds(0, NC - 1)], recv_sem.at[5])
    drain(dqv.at[pl.ds(0, 7)], send_sem.at[6])
    drain(dqv.at[pl.ds(0, 7)], recv_sem.at[6])
    drain(kv_held.at[0, pl.ds(0, NC - 1)], send_sem.at[7])
    drain(kv_held.at[1, pl.ds(0, NC - 1)], send_sem.at[8])


def fused(queries, grad_heads, w_uk, w_uv, latents, messages, w_gate, w_up, w_down):
    anywhere = pl.BlockSpec(memory_space=pl.ANY)
    whole = pl.BlockSpec(memory_space=VMEM)
    shape = jax.ShapeDtypeStruct
    return pl.pallas_call(
        fused_kernel,
        out_shape=(
            shape((TOK, 8 * HD), BF16),
            shape((TOK, 128), F32),
            shape((16, 8 * HD), F32),
            shape((16, 8 * HD), F32),
            shape((NC, 16, 128), F32),
            shape((7168, 128), BF16),
            shape((7168, 128), BF16),
            shape((128, 7168), BF16),
        ),
        in_specs=[anywhere] * 9,
        out_specs=(anywhere, whole, whole, whole, anywhere, anywhere, anywhere, anywhere),
        scratch_shapes=[
            VMEM((4, 4, 2, TOK, 512), BF16),
            VMEM((512, 4096), BF16),
            VMEM((4096, 256), F32),
            VMEM((4096, 256), F32),
            VMEM((8, 8, 256), F32),
            VMEM((512, 256), F32),
            VMEM((512, 256), F32),
            VMEM((4096, 512), F32),
            VMEM((8, TOK, HD), BF16),
            VMEM((8, TOK, HD), BF16),
            VMEM((512, HD), BF16),
            VMEM((512, HD), BF16),
            VMEM((8, TOK, HD), BF16),
            VMEM((512, HD), F32),
            VMEM((512, HD), F32),
            VMEM((2, NC, 16, HD), F32),
            VMEM((4, 4, TOK, 512), BF16),
            VMEM((4, 4, TOK, 512), BF16),
            VMEM((4, 4, TOK, 512), BF16),
            VMEM((4, 6, 64, 512), BF16),
            VMEM((4, 4, TOK, 128), BF16),
            VMEM((4, 6, 64, 128), BF16),
            VMEM((4, TOK, 128), F32),
            VMEM((7, TOK, 128), F32),
            VMEM((8, NC, 32, 128), BF16),
            VMEM((1024, 128), F32),
            VMEM((64, 7168), BF16),
            VMEM((64, 7168), BF16),
            VMEM((7168, 128), BF16),
            VMEM((7168, 128), BF16),
            VMEM((128, 7168), BF16),
            VMEM((7168, 128), BF16),
            VMEM((7168, 128), BF16),
            VMEM((128, 7168), BF16),
            VMEM((3, 64, 128), BF16),
            VMEM((8, NC, 16, 128), BF16),
            VMEM((6, NC, 16, 128), BF16),
            VMEM((NC, 16, 128), BF16),
            VMEM((NC, 16, 128), BF16),
            VMEM((NC, 16, 128), F32),
            DMA((16,)), DMA((9,)), DMA((9,)), DMA((7,)), DMA((7,)),
            DMA((14, 6)), DMA((14, 6)), DMA((8,)), DMA((7,)), DMA((7,)),
        ],
        compiler_params=pltpu.CompilerParams(
            collective_id=0, has_side_effects=True, vmem_limit_bytes=62 * 1024 * 1024
        ),
    )(queries, grad_heads, w_uk, w_uv, latents, messages, w_gate, w_up, w_down)


def on_device(
    queries, grad_heads, latents, w_uk, w_uv, moe_in, grad_out, routes, slots, gates, w_gate, w_up, w_down
):
    slot_count = NC * CAP
    destination = jnp.where(slots >= 0, routes * CAP + slots, -1)
    matches = (
        destination[:, :, None] == jnp.arange(slot_count, dtype=jnp.int32)[None, None, :]
    ).astype(F32)
    selector = jnp.sum(matches, axis=1)
    selector_low = selector.astype(BF16)
    pick = (((0,), (0,)), ((), ()))
    rows_send = lax.dot_general(selector_low, moe_in, pick, preferred_element_type=F32).astype(BF16)
    grads_send = lax.dot_general(selector_low, grad_out, pick, preferred_element_type=F32).astype(BF16)
    gate_send = jnp.sum(matches * gates.astype(F32)[:, :, None], axis=(0, 1)).astype(BF16)
    messages = jnp.concatenate(
        [
            rows_send.reshape(NC, 14, 128),
            grads_send.reshape(NC, 14, 128),
            jnp.broadcast_to(gate_send.reshape(NC, CAP, 1), (NC, CAP, 128)),
            jnp.zeros((NC, 2, 128), BF16),
        ],
        axis=1,
    )
    d_queries, d_latents, key_summed, value_summed, returned, gate_wgrad, up_wgrad, down_grad = fused(
        queries, grad_heads, w_uk, w_uv, latents, messages, w_gate[0], w_up[0], w_down[0]
    )
    d_latents = lax.dynamic_slice_in_dim(d_latents, (lax.axis_index("exp") % 2) * 64, 64, 1)
    moe_grad = jnp.dot(
        selector, returned[:, :14].reshape(slot_count, 896), precision=lax.Precision.HIGHEST
    ).astype(BF16)
    gate_grads = jnp.sum(matches * returned[:, 14:16, 0].reshape(1, 1, slot_count), axis=2)
    return (
        d_queries, d_latents, key_summed, value_summed, moe_grad, gate_grads,
        gate_wgrad[None], up_wgrad[None], down_grad[None],
    )


def solution(mesh):
    rows = P("ctx", "exp")
    in_specs = (
        rows, rows, P("ctx", None), rows, rows, rows, rows, P("ctx", None), P("ctx", None), P("ctx", None),
        P("ctx", None, "exp"), P("ctx", None, "exp"), P("ctx", "exp", None),
    )
    out_specs = (
        rows, rows, rows, rows, rows, P("ctx", None),
        P("ctx", None, "exp"), P("ctx", None, "exp"), P("ctx", "exp", None),
    )
    return jax.shard_map(on_device, mesh=mesh, in_specs=in_specs, out_specs=out_specs, check_vma=False)
```

time: 213 us -> 158 us (0.74); the launches traced: 213 us -> 155 us
  Pallas kernels: 167 us -> 135 us
  matrix products: 16.9 us -> 2.55 us
  local copies, waits for them, and re-layouts: 22.5 us -> 13.8 us
  other arithmetic: 5.57 us -> 3.08 us
    pallas_call x3 -> x1, Pallas kernels: 167 us -> 135 us  [fused(): pl.pallas_call(fused_kernel, out_shape=(shape((TOK, 8 * HD), BF16), shape...]
    dot_general x8 -> x0, matrix products: 13.4 us -> none  [the longest x1 2.53 us: on_device(): lax.dot_general(grads_flat, down_weight, last, preferred_element_type=F32)]
    reshape x4 -> x0, local copies, waits for them, and re-layouts: 8.48 us -> none  [the longest x2 5.02 us: full(): return part.transpose(1, 2, 0, 3, 4).reshape(slot_count, 8 * 896)]
    unnamed x20 -> x17, local copies, waits for them, and re-layouts: 3.45 us -> 10 us
    transpose x3 -> x0, local copies, waits for them, and re-layouts: 4.64 us -> none  [the longest x2 2.75 us: full(): return part.transpose(1, 2, 0, 3, 4).reshape(slot_count, 8 * 896)]
where the time goes in v2:
time: 158 us; the launch traced here: 155 us
  Pallas kernels  135 us (85%)
  local copies, waits for them, and re-layouts  13.8 us (9%)
  other arithmetic  3.08 us (2%)
  matrix products  2.55 us (2%)
    pallas_call x1, Pallas kernels, fused(): pl.pallas_call(fused_kernel, out_shape=(shape((TOK, 8 * HD), BF16), shape...  135 us
    unnamed x17, local copies, waits for them, and re-layouts  10 us

profile of v2, /device:TPU:8, one launch (start us, length us, event | category | flops | bytes accessed | tf_op | source)
XLA Modules:
  0.0 155.4 jit_solution(9889805654264104566)
XLA Ops:
  0.6 0.0 copy-start
  0.7 0.1 pad.3.clone
  0.8 0.7 add_select_fusion
  1.5 0.7 convert_element_type.32
  2.2 0.1 convert_reduce_fusion
  2.3 0.1 convert_element_type.34
  2.4 0.1 broadcast_in_dim.25
  2.5 0.0 copy-done
  2.5 0.2 convolution_convert_fusion.1
  2.7 0.1 reshape.38
  2.9 1.1 convolution_convert_fusion.2
  4.0 0.1 reshape.37
  4.1 0.8 maximum_maximum_fusion.moe_ref
  5.0 135.2 %shard_map.196 = (bf16[128,1024]{1,0:T(8,128)(2,1)}, f32[128,128]{1,0:T(8,128)}, f32[16,1024]{1,0:T(8,128)}, f32[16,1024]{1,0:T(8,128)}, f32[32,16,128]{2,1,0:T(...) custom-call(bf16[128,1024]{1,0:T(8,128)(2,1)} %q_ref.1, ...), custom_call_target="tpu_custom_call" | custom-call | tf_op jit(solution)/shard_map/pallas_call | solution.py:596
  140.2 0.0 copy-start.4
  140.2 0.0 copy-start.3
  140.2 1.1 slice_reduce_fusion
  141.4 0.1 mul.32
  141.5 0.7 select_reduce_fusion
  142.2 0.9 constant_dynamic-slice_fusion
  143.1 0.7 copy.28
  143.8 1.0 reshape.39
  144.8 1.3 convolution_convert_fusion
  146.1 1.7 %copy.35 = bf16[128,1024]{1,0:T(8,128)(2,1)} copy(bf16[128,1024]{1,0:T(8,128)(2,1)} %get-tuple-element.63) | data formatting | bytes 524288
  147.7 1.5 copy.36
  149.2 0.0 copy-done.4
  149.2 0.6 copy.37
  149.9 0.0 copy-done.3
  149.9 0.0 copy-start.2
  149.9 1.2 copy.38
  151.1 0.9 copy-done.2
  152.0 0.0 copy-start.1
  152.0 1.2 copy.39
  153.2 0.9 copy-done.1
  154.2 1.2 copy.40
  (1 shorter events, 0.0 us)
Async XLA Ops:
  0.6 1.9 %copy-start = (bf16[128,896]{1,0:T(8,128)(2,1)S(1)}, bf16[128,896]{1,0:T(8,128)(2,1)}, u32[]{:S(2)}) copy-start(bf16[128,896]{1,0:T(8,128)(2,1)} %param.19) | copy-start | bytes 688132
  140.2 9.0 %copy-start.4 = (f32[16,1024]{1,0:T(8,128)S(1)}, f32[16,1024]{1,0:T(8,128)}, u32[]{:S(2)}) copy-start(f32[16,1024]{1,0:T(8,128)} %get-tuple-element.66) | copy-start | bytes 196612
  140.2 9.6 %copy-start.3 = (bf16[7168,128]{1,0:T(8,128)(2,1)S(1)}, bf16[7168,128]{1,0:T(8,128)(2,1)}, u32[]{:S(2)}) copy-start(bf16[7168,128]{1,0:T(8,128)(2,1)} %get-tuple-element.22) | copy-start | bytes 5505028
  149.9 2.2 %copy-start.2 = (bf16[7168,128]{1,0:T(8,128)(2,1)S(1)}, bf16[7168,128]{1,0:T(8,128)(2,1)}, u32[]{:S(2)}) copy-start(bf16[7168,128]{1,0:T(8,128)(2,1)} %get-tuple-element.23) | copy-start | bytes 5505028
  152.0 2.2 %copy-start.1 = (bf16[128,7168]{1,0:T(8,128)(2,1)S(1)}, bf16[128,7168]{1,0:T(8,128)(2,1)}, u32[]{:S(2)}) copy-start(bf16[128,7168]{1,0:T(8,128)(2,1)} %get-tuple-element.24) | copy-start | bytes 5505028

commit v3 on v2

--- a/solution.py
+++ b/solution.py
@@ -84,11 +84,14 @@
         drain(at(after, 1), recv_sem.at[3])
         send(at(after, 1), at(after, 1), send_sem.at[5], recv_sem.at[5], left)
 
-    def last():
+    def last(arrived=lambda k, q: None):
         drain(at(before, 1), recv_sem.at[1])
+        arrived(1, before)
         drain(at(after, 0), recv_sem.at[2])
+        arrived(2, after)
         drain(at(other, 0), recv_sem.at[4])
         drain(at(other, 1), recv_sem.at[5])
+        arrived(3, other)
         for k in range(6):
             drain(at(pos, 0), send_sem.at[k])
 
@@ -137,24 +140,29 @@
 def fused_kernel(
     q_ref, g_ref, wk_ref, wv_ref, lat_ref, moe_ref, wg_ref, wu_ref, wd_ref,
     dqo, dlo, kgo, vgo, mo, gwgo, gwuo, gwdo,
-    lat, lat_t, probs, dprob, tops, o_t, dq_t, dlat, qv, gv, wkv, wvv, dqv, kgv, vgv, kv_held,
+    lat, lat_t, probs, dprob, tops, o_t, dq_t, dlat, qv, gv, w4, wkv, wvv, dqv, kgv, vgv, kq, kr, ks, kv_held,
     core_out, core_held, part, x_held, y_part, y_held, z_part, z_held,
-    rows, spread, xs, ys, wg, wu, wd, gwg, gwu, gwd, dh, m_part, m_held, twin_part, twin_held, m_send,
+    rows, spread, xs, ys, wg, wu, wd, gwg, gwu, gwd, dh, m_part, m_held, m_send, gate_sum,
     own_sem, send_sem, recv_sem, z_send, z_recv, ring_send, ring_recv, core_sem, last_send, last_recv,
+    piece_send, piece_recv, local_send, local_recv,
 ):
     at = Place()
     c, e = at.c, at.e
     left_x, right_x = at.ctx(at.z, (at.x + 3) % 4, at.core), at.ctx(at.z, (at.x + 1) % 4, at.core)
     left_y, right_y = at.exp((at.y + 3) % 4, at.zh), at.exp((at.y + 1) % 4, at.zh)
-    twin, sibling = at.exp(at.y, 1 - at.zh), at.ctx(at.z, at.x, 1 - at.core)
-    far = [(((at.z + k) % 4) * 8 + c % 8, at.y * 2 + 1 - at.zh) for k in range(1, 4)]
-    greet((left_y, right_y, twin, *far), ((NC - 1, lambda k: ((c + 1 + k) % NC, e)),))
+    sibling = at.ctx(at.z, at.x, 1 - at.core)
+    e_far = at.y * 2 + 1 - at.zh
+    greet(
+        [at.exp((at.y + k) % 4, at.zh) for k in range(1, 4)],
+        ((NC - 1, lambda k: ((c + 1 + k) % NC, e)), (NC, lambda k: ((c + k) % NC, e_far))),
+    )
 
     def lanes(h):
         return pl.ds(pl.multiple_of(h * HD, HD), HD)
 
-    def rows16(d):
-        return pl.ds(pl.multiple_of(d * 16, 16), 16)
+    def local(k):
+        p = (c % 4 + k) % 4
+        return (4 * at.i + p, e), p + (at.i % 2) * (3 - 2 * p)
 
     def gather_ring(n, pos, left, right, ref_at):
         return ring_gather(ref_at, pos, left, right, ring_send.at[n], ring_recv.at[n])
@@ -167,8 +175,8 @@
         pltpu.make_async_copy(lat_ref.at[:, lanes(at.y)], lat.at[at.z, at.x, at.core, :, lanes(at.y)], own_sem.at[1]),
         pltpu.make_async_copy(q_ref.at[:, lanes(at.i)], qv.at[at.i], own_sem.at[2]),
         pltpu.make_async_copy(g_ref.at[:, lanes(at.i)], gv.at[at.i], own_sem.at[3]),
-        pltpu.make_async_copy(wk_ref.at[:, lanes(at.i)], wkv.at[rows16(c)], own_sem.at[4]),
-        pltpu.make_async_copy(wv_ref.at[:, lanes(at.i)], wvv.at[rows16(c)], own_sem.at[5]),
+        pltpu.make_async_copy(wk_ref.at[:, lanes(at.i)], w4.at[at.r, 0, at.i], own_sem.at[4]),
+        pltpu.make_async_copy(wv_ref.at[:, lanes(at.i)], w4.at[at.r, 1, at.i], own_sem.at[5]),
         pltpu.make_async_copy(wg_ref, wg, own_sem.at[6]),
         pltpu.make_async_copy(wu_ref, wu, own_sem.at[7]),
         pltpu.make_async_copy(wd_ref, wd, own_sem.at[8]),
@@ -185,9 +193,16 @@
     def send_rows(k, carry):
         d = (c + 1 + k) % NC
         send(moe_ref.at[d], rows.at[e, c], send_sem.at[0], recv_sem.at[0], (d, e))
+        send(moe_ref.at[d], rows.at[e, c], send_sem.at[9], recv_sem.at[9], (d, e_far))
         return carry
 
-    lax.fori_loop(0, NC - 1, send_rows, 0)
+
+    def send_weights(k, carry):
+        i = (at.i + 1 + k) % 8
+        d = (at.member(i), e)
+        send(wk_ref.at[:, lanes(i)], w4.at[at.r, 0, at.i], send_sem.at[3], recv_sem.at[3], d)
+        send(wv_ref.at[:, lanes(i)], w4.at[at.r, 1, at.i], send_sem.at[4], recv_sem.at[4], d)
+        return carry
 
     def send_heads(k, carry):
         i = (at.i + 1 + k) % 8
@@ -196,15 +211,6 @@
         send(g_ref.at[:, lanes(i)], gv.at[at.i], send_sem.at[2], recv_sem.at[2], d)
         return carry
 
-    lax.fori_loop(0, 7, send_heads, 0)
-
-    def send_weights(k, carry):
-        d = (c + 1 + k) % NC
-        send(wk_ref.at[:, lanes(d // 4)], wkv.at[rows16(c)], send_sem.at[3], recv_sem.at[3], (d, e))
-        send(wv_ref.at[:, lanes(d // 4)], wvv.at[rows16(c)], send_sem.at[4], recv_sem.at[4], (d, e))
-        return carry
-
-    lax.fori_loop(0, NC - 1, send_weights, 0)
     for k in (6, 7, 8):
         own[k].start()
 
@@ -217,30 +223,61 @@
     xb = gather_ring(3, at.x, left_x, right_x, lambda q, h: lat.at[2 + h, q, at.core])
     xa[0]()
     yb[0]()
+    lax.fori_loop(0, 7, send_heads, 0)
+    lax.fori_loop(0, 7, send_weights, 0)
     xa[1]()
     yb[1]()
+
+    def piece_a(k, q):
+        ref = lat.at[pl.ds(0, 2), :, at.core, :, lanes(q)]
+        send(ref, ref, piece_send.at[k], piece_recv.at[k], sibling)
+
+    def piece_b(k, q):
+        ref = lat.at[pl.ds(2, 2), q, at.core]
+        send(ref, ref, piece_send.at[4 + k], piece_recv.at[4 + k], sibling)
+
     xa[2]()
     ya[0]()
+    piece_a(0, at.y)
     yb[2]()
     xb[0]()
-    own[0].wait()
-    drain(rows.at[e, pl.ds(0, NC - 1)], recv_sem.at[0])
-    twin_in = send(rows.at[e], rows.at[e], z_send.at[3], z_recv.at[3], twin)
+    piece_b(0, at.x)
+    lax.fori_loop(0, NC - 1, send_rows, 0)
+    send(moe_ref.at[c], rows.at[e, c], send_sem.at[9], recv_sem.at[9], (c, e_far))
     ya[1]()
     xb[1]()
-    ya[2]()
-    core_a = send(lat.at[pl.ds(0, 2), :, at.core], lat.at[pl.ds(0, 2), :, at.core], z_send.at[4], z_recv.at[4], sibling)
-    xb[2]()
-    core_b = send(lat.at[pl.ds(2, 2), :, at.core], lat.at[pl.ds(2, 2), :, at.core], z_send.at[5], z_recv.at[5], sibling)
-    for k in (2, 3, 4, 5):
+    for k in (4, 5):
+        own[k].wait()
+    for k in (3, 4):
+        drain(w4.at[at.r, k - 3, pl.ds(0, 7)], recv_sem.at[k])
+    for k in range(1, 4):
+        send(w4.at[at.r], w4.at[at.r], local_send.at[k - 1], local_recv.at[k - 1], local(k)[0])
+    ya[2](piece_a)
+    xb[2](piece_b)
+    for k in range(3):
+        drain(w4.at[at.r], local_recv.at[k])
+    for i in range(8):
+        for p in range(4):
+            group = p if i % 2 == 0 else 3 - p
+            rows16 = pl.ds(16 * (4 * i + p), 16)
+            wkv[rows16] = w4[group, 0, i]
+            wvv[rows16] = w4[group, 1, i]
+    for k in (2, 3):
         own[k].wait()
     for k, ref in ((1, qv), (2, gv)):
         drain(ref.at[pl.ds(0, 7)], recv_sem.at[k])
-    for k, ref in ((3, wkv), (4, wvv)):
-        drain(ref.at[pl.ds(0, 16 * (NC - 1))], recv_sem.at[k])
-    core_a.wait_recv()
+
+    my = gather_ring(12, at.y, left_y, right_y, lambda q, h: rows.at[2 * q + h])
+    mr = scatter_ring(13, at.y, left_y, right_y, lambda q, h: m_part.at[2 * q + h], m_held)
+
+    def rows_here():
+        own[0].wait()
+        drain(rows.at[e, pl.ds(0, NC - 1)], recv_sem.at[0])
+        drain(rows.at[e_far], recv_sem.at[9])
+        my[0]()
 
     scale = HD**-0.5
+    fast = scale * 1.4426950408889634
     contract_last = (((1,), (1,)), ((), ()))
     contract_first = (((0,), (0,)), ((), ()))
     width = 512
@@ -251,63 +288,84 @@
     def keys_at(t):
         return lat[t // 2, pl.ds(2 * (t % 2), 2)].reshape(width, 512)
 
-    def turn(t, carry):
-        lat_t[:, tile(t)] = keys_at(t).T
-        return carry
-
-    lax.fori_loop(0, 4, turn, 0)
-    core_b.wait_recv()
-    lax.fori_loop(4, 8, turn, 0)
+    def pieces(first):
+        for k in range(first, first + 4):
+            drain(lat.at[pl.ds(0, 2), :, 0, :, pl.ds(0, 128)], piece_recv.at[k])
+
+    pieces(0)
     column = lax.broadcasted_iota(jnp.int32, (1, 256), 1)
     key_at = lax.broadcasted_iota(jnp.int32, (width, 1), 0)
 
-    def chunk(j):
+    def chunk(j, after_score=(), after_output=()):
         q, g = qv[2 * j : 2 * j + 2].reshape(256, HD), gv[2 * j : 2 * j + 2].reshape(256, HD)
         q_lat = lax.dot_general(q, wkv[...], contract_last, preferred_element_type=F32).astype(BF16)
         g_lat = lax.dot_general(g, wvv[...], contract_last, preferred_element_type=F32).astype(BF16)
         position = column + jnp.where(column < TOK, (8 * j + at.r) * TOK, (8 * j + 6 - at.r) * TOK)
+
+        def score(b, state, masked):
+            top, total = state
+            raw = []
+            for t in (2 * b, 2 * b + 1):
+                keys = keys_at(t)
+                if j == 3:
+                    lat_t[:, tile(t)] = keys.T
+                s = lax.dot_general(keys, q_lat, contract_last, preferred_element_type=F32)
+                if masked:
+                    s = jnp.where(key_at + t * width <= position, s, -jnp.inf)
+                raw.append(s)
+                dprob[tile(t), :] = lax.dot_general(keys, g_lat, contract_last, preferred_element_type=F32)
+            new_top = jnp.maximum(top, jnp.max(jnp.maximum(raw[0], raw[1]), axis=0, keepdims=True))
+            total = total * jnp.exp2((top - new_top) * fast)
+            for u in range(2):
+                weight = jnp.exp2((raw[u] - new_top) * fast)
+                probs[tile(2 * b + u), :] = weight
+                total = total + jnp.sum(weight, axis=0, keepdims=True)
+            tops[b] = jnp.broadcast_to(new_top, (8, 256))
+            return new_top, total
+
+        state = (jnp.full((1, 256), -1e30, F32), jnp.zeros((1, 256), F32))
+        if j == 3:
+            state = lax.fori_loop(0, 2, lambda b, s: score(b, s, False), state)
+            pieces(4)
+            state = score(2, state, False)
+        elif j > 0:
+            state = lax.fori_loop(0, j, lambda b, s: score(b, s, False), state)
+        top, total = score(j, state, True)
+        inverse = 1.0 / total
+        for step in after_score:
+            step()
         o_t[...] = jnp.zeros_like(o_t)
         dq_t[...] = jnp.zeros_like(dq_t)
 
-        def score(t, state, masked):
-            top, total = state
-            keys = keys_at(t)
-            s = lax.dot_general(keys, q_lat, contract_last, preferred_element_type=F32) * scale
-            if masked:
-                s = jnp.where(key_at + t * width <= position, s, -jnp.inf)
-            new_top = jnp.maximum(top, jnp.max(s, axis=0, keepdims=True))
-            weight = jnp.exp(s - new_top)
-            probs[tile(t), :] = weight
-            tops[t] = jnp.broadcast_to(new_top, (8, 256))
-            dprob[tile(t), :] = lax.dot_general(keys, g_lat, contract_last, preferred_element_type=F32)
-            total = total * jnp.exp(top - new_top) + jnp.sum(weight, axis=0, keepdims=True)
-            return new_top, total
-
-        state = (jnp.full((1, 256), -1e30, F32), jnp.zeros((1, 256), F32))
-        state = lax.fori_loop(0, 2 * j, lambda t, s: score(t, s, False), state)
-        top, total = lax.fori_loop(2 * j, 2 * j + 2, lambda t, s: score(t, s, True), state)
-        inverse = 1.0 / total
-
-        def output(t, delta):
-            prob = probs[tile(t), :] * (jnp.exp(tops[t][0:1, :] - top) * inverse)
-            prob_low = prob.astype(BF16)
-            probs[tile(t), :] = prob
-            o_t[...] += jnp.dot(lat_t[:, tile(t)], prob_low, preferred_element_type=F32)
-            return delta + jnp.sum(prob_low.astype(F32) * dprob[tile(t), :], axis=0, keepdims=True)
-
-        delta = lax.fori_loop(0, 2 * j + 2, output, jnp.zeros((1, 256), F32))
-
-        def gradient(t, carry):
-            prob = probs[tile(t), :]
-            dscore = (prob * (dprob[tile(t), :] - delta) * scale).astype(BF16)
-            dq_t[...] += jnp.dot(lat_t[:, tile(t)], dscore, preferred_element_type=F32)
-            step = jnp.dot(dscore, q_lat, preferred_element_type=F32) + jnp.dot(
-                prob.astype(BF16), g_lat, preferred_element_type=F32
-            )
-            dlat[tile(t), :] = step if j == 3 else dlat[tile(t), :] + step
+        def output(b, delta):
+            factor = jnp.exp2((tops[b][0:1, :] - top) * fast) * inverse
+            sum_o = o_t[...]
+            for t in (2 * b, 2 * b + 1):
+                prob_low = (probs[tile(t), :] * factor).astype(BF16)
+                sum_o = sum_o + jnp.dot(lat_t[:, tile(t)], prob_low, preferred_element_type=F32)
+                delta = delta + jnp.sum(prob_low.astype(F32) * dprob[tile(t), :], axis=0, keepdims=True)
+            o_t[...] = sum_o
+            return delta
+
+        delta = lax.fori_loop(0, j + 1, output, jnp.zeros((1, 256), F32))
+        for step in after_output:
+            step()
+
+        def gradient(b, carry):
+            factor = jnp.exp2((tops[b][0:1, :] - top) * fast) * inverse
+            sum_q = dq_t[...]
+            for t in (2 * b, 2 * b + 1):
+                prob = probs[tile(t), :] * factor
+                dscore = (prob * (dprob[tile(t), :] - delta) * scale).astype(BF16)
+                sum_q = sum_q + jnp.dot(lat_t[:, tile(t)], dscore, preferred_element_type=F32)
+                step = jnp.dot(dscore, q_lat, preferred_element_type=F32) + jnp.dot(
+                    prob.astype(BF16), g_lat, preferred_element_type=F32
+                )
+                dlat[tile(t), :] = step if j == 3 else dlat[tile(t), :] + step
+            dq_t[...] = sum_q
             return carry
 
-        lax.fori_loop(0, 2 * j + 2, gradient, 0)
+        lax.fori_loop(0, j + 1, gradient, 0)
         dq_low = dq_t[...].astype(BF16)
         dq = lax.dot_general(dq_low, wkv[...], contract_first, preferred_element_type=F32).astype(BF16)
         dqv[2 * j : 2 * j + 2] = dq.reshape(2, TOK, HD)
@@ -315,6 +373,16 @@
         vg = jnp.dot(o_t[...].astype(BF16), g, preferred_element_type=F32)
         kgv[...] = kg if j == 3 else kgv[...] + kg
         vgv[...] = vg if j == 3 else vgv[...] + vg
+        for n in (2 * j, 2 * j + 1):
+            block = dqo.at[:, lanes(at.i)]
+
+            @pl.when(at.i == n)
+            def _():
+                pltpu.make_async_copy(dqv.at[n], block, own_sem.at[12]).start()
+
+            @pl.when(at.i != n)
+            def _():
+                send(dqv.at[n], block, send_sem.at[6], recv_sem.at[6], (at.member(n), e))
 
     class Reduce:
         def __init__(self, b):
@@ -323,10 +391,6 @@
             self.x_ring = scatter_ring(
                 4 + b, at.x, left_x, right_x,
                 lambda q, h: part.at[b, q, pl.ds(64 * h, 64)], x_held.at[b],
-            )
-            self.y_ring = scatter_ring(
-                8 + b, at.y, left_y, right_y,
-                lambda q, h: y_part.at[b, q, pl.ds(64 * h, 64)], y_held.at[b],
             )
 
         def block(self, x, core):
@@ -366,24 +430,22 @@
                 ).astype(BF16)
                 for q in range(4):
                     y_part[b, q, half] = total[:, q * 128 : (q + 1) * 128]
-            self.y_ring[0]()
-
-        def y2(self):
-            self.y_ring[1]()
+            for k in range(1, 4):
+                q = (at.y + k) % 4
+                send(
+                    y_part.at[b, q], y_held.at[b, k - 1], ring_send.at[8 + b, k], ring_recv.at[8 + b, k],
+                    at.exp(q, at.zh),
+                )
 
         def y3(self):
             b = self.b
-            self.y_ring[2]()
-            for h in range(2):
-                half = pl.ds(64 * h, 64)
-                z_part[b, half] = (
-                    y_part[b, at.y, half].astype(F32) + y_held[b, 2 + h].astype(F32) + y_held[b, 4 + h].astype(F32)
-                )
+            total = y_part[b, at.y].astype(F32)
+            for k in range(3):
+                drain(y_held.at[b, k], ring_recv.at[8 + b, k + 1])
+                total = total + y_held[b, k].astype(F32)
+            z_part[b] = total.astype(BF16)
 
     rs = [Reduce(b) for b in range(4)]
-
-    my = gather_ring(12, at.y, left_y, right_y, lambda q, h: rows.at[2 * q + h])
-    mr = scatter_ring(13, at.y, left_y, right_y, lambda q, h: m_part.at[2 * q + h], m_held)
 
     def slice_lanes(n, f):
         return pl.ds(pl.multiple_of(n * 896 + f * 128, 128), 128)
@@ -424,8 +486,11 @@
         dh[0] = (gate * act).astype(BF16)
         dh[1] = (scaled * h2 * s * (1.0 + h1 * (1.0 - s))).astype(BF16)
         dh[2] = (scaled * h1 * s).astype(BF16)
+        gate_sum[...] = gate_part
+
+    def experts_back():
         for k in range(2):
-            spread[pl.ds(14 + k, 32, stride=16), :] = gate_part[32 * k : 32 * k + 32]
+            spread[pl.ds(14 + k, 32, stride=16), :] = gate_sum[32 * k : 32 * k + 32, :]
 
         def back(n, carry):
             dx = lax.dot_general(dh[1], wg[slice_all(n), :], contract_last, preferred_element_type=F32)
@@ -465,128 +530,128 @@
     def y_total(h, k):
         return m_part[2 * at.y + h, k].astype(F32) + m_held[2 + h, k].astype(F32) + m_held[4 + h, k].astype(F32)
 
-    def twin_out(k, carry):
-        twin_part[k] = y_total(1 - at.zh, k).astype(BF16)
-        return carry
-
-    def twin_sum(k, carry):
-        m_send[k] = y_total(at.zh, k) + twin_held[k].astype(F32)
+    def sum_rows(k, carry):
+        for h in range(2):
+            m_send[h, k] = y_total(h, k).astype(BF16)
         return carry
 
     def send_back(k, carry):
         d = (c + 1 + k) % NC
-        send(m_send.at[d], mo.at[c], send_sem.at[5], recv_sem.at[5], (d, e))
+        send(m_send.at[at.zh, d], mo.at[at.zh, c], send_sem.at[5], recv_sem.at[5], (d, e))
+        send(m_send.at[1 - at.zh, d], mo.at[at.zh, c], send_sem.at[8], recv_sem.at[8], (d, e_far))
         return carry
 
-    def return_heads(k, carry):
-        i = (at.i + 1 + k) % 8
-        send(dqv.at[i], dqo.at[:, lanes(at.i)], send_sem.at[6], recv_sem.at[6], (at.member(i), e))
-        return carry
-
-    def return_weights(k, carry):
-        d = (c + 1 + k) % NC
-        send(kgv.at[rows16(d)], kv_held.at[0, c], send_sem.at[7], recv_sem.at[7], (d, e))
-        send(vgv.at[rows16(d)], kv_held.at[1, c], send_sem.at[8], recv_sem.at[8], (d, e))
-        return carry
-
-    twin_in.wait_recv()
-    my[0]()
-    chunk(3)
+    def rows_back():
+        mr[2]()
+        lax.fori_loop(0, NC, sum_rows, 0)
+        pltpu.make_async_copy(m_send.at[at.zh, c], mo.at[at.zh, c], own_sem.at[15]).start()
+        lax.fori_loop(0, NC - 1, send_back, 0)
+        send(m_send.at[1 - at.zh, c], mo.at[at.zh, c], send_sem.at[8], recv_sem.at[8], (c, e_far))
+
+    def spread_weights():
+        for i in range(8):
+            for p in range(4):
+                group = p if i % 2 == 0 else 3 - p
+                rows16 = pl.ds(16 * (4 * i + p), 16)
+                kq[group, i, 0] = kgv[rows16]
+                kq[group, i, 1] = vgv[rows16]
+        for k in range(1, 4):
+            device, group = local(k)
+            send(kq.at[group], kr.at[k - 1], local_send.at[2 + k], local_recv.at[2 + k], device)
+
+    def return_weights():
+        for k in range(3):
+            drain(kr.at[k], local_recv.at[3 + k])
+
+        def one(i, carry):
+            ks[i] = (kq[at.r, i] + kr[0, i]) + (kr[1, i] + kr[2, i])
+            return carry
+
+        lax.fori_loop(0, 8, one, 0)
+        pltpu.make_async_copy(ks.at[at.i], kv_held.at[at.i], own_sem.at[13]).start()
+
+        def out(k, carry):
+            i = (at.i + 1 + k) % 8
+            send(ks.at[i], kv_held.at[at.i], send_sem.at[7], recv_sem.at[7], (at.member(i), e))
+            return carry
+
+        lax.fori_loop(0, 7, out, 0)
+
+    kept = []
+
+    chunk(3, after_output=(rows_here,))
     rs[3].to_core()
-    my[1]()
-    chunk(2)
-    rs[3].x1()
+    chunk(2, after_score=(rs[3].x1, my[1]), after_output=(rs[3].x2,))
     rs[2].to_core()
+    chunk(1, after_score=(rs[2].x1, rs[3].x3), after_output=(rs[2].x2,))
+    rs[1].to_core()
+    rs[3].y3()
+    chunk(0, after_score=(rs[1].x1, rs[2].x3), after_output=(rs[1].x2,))
+    rs[0].to_core()
+    spread_weights()
     my[2]()
     experts()
+    rs[0].x1()
+    rs[2].y3()
+    rs[1].x3()
+    experts_back()
     mr[0]()
-    chunk(1)
-    rs[3].x2()
-    rs[2].x1()
-    rs[1].to_core()
+    rs[0].x2()
+    return_weights()
+    rs[1].y3()
+    kept.append(down_grads())
     mr[1]()
-    chunk(0)
-    rs[0].to_core()
-    lax.fori_loop(0, 7, return_heads, 0)
-    lax.fori_loop(0, NC - 1, return_weights, 0)
-    kept = [
-        pltpu.make_async_copy(dqv.at[at.i], dqo.at[:, lanes(at.i)], own_sem.at[12]),
-        pltpu.make_async_copy(kgv.at[rows16(c)], kv_held.at[0, c], own_sem.at[13]),
-        pltpu.make_async_copy(vgv.at[rows16(c)], kv_held.at[1, c], own_sem.at[14]),
-    ]
-    for copy in kept:
-        copy.start()
-    mr[2]()
-    lax.fori_loop(0, NC, twin_out, 0)
-    twin_back = send(twin_part, twin_held, z_send.at[6], z_recv.at[6], twin)
-    rs[2].x2()
-    rs[1].x1()
-    rs[3].x3()
-    rs[0].x1()
-    kept.append(down_grads())
-    rs[1].x2()
-    rs[3].y2()
-    rs[2].x3()
-    rs[0].x2()
-    twin_back.wait_recv()
-    lax.fori_loop(0, NC, twin_sum, 0)
-    kept.append(pltpu.make_async_copy(m_send.at[c], mo.at[c], own_sem.at[15]))
-    kept[-1].start()
-    lax.fori_loop(0, NC - 1, send_back, 0)
-    rs[1].x3()
     rs[0].x3()
-    rs[3].y3()
-    rs[2].y2()
     kept.append(weight_grads(gwg, 1, gwgo, own_sem.at[9]))
-    rs[1].y2()
-    rs[0].y2()
-    kept.append(weight_grads(gwu, 2, gwuo, own_sem.at[10]))
-    rs[2].y3()
-    rs[1].y3()
+    rows_back()
     rs[0].y3()
     for k in range(1, 8):
         place = (at.zh * 4 + at.z + k) % 8
         z = place % 4
         device = (z * 8 + c % 8, at.y * 2 + place // 4)
         send(z_part.at[z], z_held.at[k - 1], last_send.at[k - 1], last_recv.at[k - 1], device)
-
-    kept[1].wait()
-    kept[2].wait()
-    drain(kv_held.at[0, pl.ds(0, NC - 1)], recv_sem.at[7])
-    drain(kv_held.at[1, pl.ds(0, NC - 1)], recv_sem.at[8])
+    kept.append(weight_grads(gwu, 2, gwuo, own_sem.at[10]))
+
+    drain(ks.at[0], own_sem.at[13])
+    drain(ks.at[pl.ds(0, 7)], recv_sem.at[7])
     for n, out in ((0, kgo), (1, vgo)):
         for h in range(8):
-            out[:, h * HD : (h + 1) * HD] = (kv_held[n, 4 * h] + kv_held[n, 4 * h + 1]) + (
-                kv_held[n, 4 * h + 2] + kv_held[n, 4 * h + 3]
-            )
-    total = z_part[at.z]
+            out[:, h * HD : (h + 1) * HD] = kv_held[h, n]
+    total = z_part[at.z].astype(F32)
     for k in range(7):
         drain(z_held.at[k], last_recv.at[k])
-        total = total + z_held[k]
-    dlo[...] = total
-
-    kept[0].wait()
-    for copy in kept[3:]:
+        total = total + z_held[k].astype(F32)
+    dlo[...] = jnp.where(at.zh == 0, total[:, :64], total[:, 64:]).T
+
+    for copy in kept:
         copy.wait()
     for k in range(7):
         drain(z_held.at[k], last_send.at[k])
     for b in range(4):
         rs[b].copy.wait_send()
-    for copy in (twin_in, twin_back, core_a, core_b):
-        copy.wait_send()
+        for k in range(3):
+            drain(y_held.at[b, k], ring_send.at[8 + b, k + 1])
     for k in range(3):
         drain(lat_own, z_send.at[k])
+        drain(w4.at[at.r], local_send.at[k])
+        drain(kr.at[k], local_send.at[3 + k])
+    for k in range(8):
+        drain(lat.at[pl.ds(0, 2), :, 0, :, pl.ds(0, 128)], piece_send.at[k])
     drain(rows.at[e, pl.ds(0, NC - 1)], send_sem.at[0])
     for k, ref in ((1, qv), (2, gv)):
         drain(ref.at[pl.ds(0, 7)], send_sem.at[k])
-    for k, ref in ((3, wkv), (4, wvv)):
-        drain(ref.at[pl.ds(0, 16 * (NC - 1))], send_sem.at[k])
-    drain(m_send.at[pl.ds(0, NC - 1)], send_sem.at[5])
-    drain(m_send.at[pl.ds(0, NC - 1)], recv_sem.at[5])
+    for k in (3, 4):
+        drain(w4.at[at.r, k - 3, pl.ds(0, 7)], send_sem.at[k])
+    drain(m_send.at[0, 0], own_sem.at[15])
+    drain(m_send.at[0, pl.ds(0, NC - 1)], send_sem.at[5])
+    drain(m_send.at[0, pl.ds(0, NC - 1)], recv_sem.at[5])
+    drain(m_send.at[0], send_sem.at[8])
+    drain(m_send.at[0], recv_sem.at[8])
+    drain(rows.at[e], send_sem.at[9])
+    drain(dqv.at[0], own_sem.at[12])
     drain(dqv.at[pl.ds(0, 7)], send_sem.at[6])
     drain(dqv.at[pl.ds(0, 7)], recv_sem.at[6])
-    drain(kv_held.at[0, pl.ds(0, NC - 1)], send_sem.at[7])
-    drain(kv_held.at[1, pl.ds(0, NC - 1)], send_sem.at[8])
+    drain(ks.at[pl.ds(0, 7)], send_sem.at[7])
 
 
 def fused(queries, grad_heads, w_uk, w_uv, latents, messages, w_gate, w_up, w_down):
@@ -597,10 +662,10 @@
         fused_kernel,
         out_shape=(
             shape((TOK, 8 * HD), BF16),
-            shape((TOK, 128), F32),
+            shape((64, TOK), F32),
             shape((16, 8 * HD), F32),
             shape((16, 8 * HD), F32),
-            shape((NC, 16, 128), F32),
+            shape((2, NC, 16, 128), BF16),
             shape((7168, 128), BF16),
             shape((7168, 128), BF16),
             shape((128, 7168), BF16),
@@ -618,20 +683,24 @@
             VMEM((4096, 512), F32),
             VMEM((8, TOK, HD), BF16),
             VMEM((8, TOK, HD), BF16),
+            VMEM((4, 2, 8, 16, HD), BF16),
             VMEM((512, HD), BF16),
             VMEM((512, HD), BF16),
             VMEM((8, TOK, HD), BF16),
             VMEM((512, HD), F32),
             VMEM((512, HD), F32),
-            VMEM((2, NC, 16, HD), F32),
+            VMEM((4, 8, 2, 16, HD), F32),
+            VMEM((3, 8, 2, 16, HD), F32),
+            VMEM((8, 2, 16, HD), F32),
+            VMEM((8, 2, 16, HD), F32),
             VMEM((4, 4, TOK, 512), BF16),
             VMEM((4, 4, TOK, 512), BF16),
             VMEM((4, 4, TOK, 512), BF16),
             VMEM((4, 6, 64, 512), BF16),
             VMEM((4, 4, TOK, 128), BF16),
-            VMEM((4, 6, 64, 128), BF16),
-            VMEM((4, TOK, 128), F32),
-            VMEM((7, TOK, 128), F32),
+            VMEM((4, 3, TOK, 128), BF16),
+            VMEM((4, TOK, 128), BF16),
+            VMEM((7, TOK, 128), BF16),
             VMEM((8, NC, 32, 128), BF16),
             VMEM((1024, 128), F32),
             VMEM((64, 7168), BF16),
@@ -645,16 +714,90 @@
             VMEM((3, 64, 128), BF16),
             VMEM((8, NC, 16, 128), BF16),
             VMEM((6, NC, 16, 128), BF16),
-            VMEM((NC, 16, 128), BF16),
-            VMEM((NC, 16, 128), BF16),
-            VMEM((NC, 16, 128), F32),
-            DMA((16,)), DMA((9,)), DMA((9,)), DMA((7,)), DMA((7,)),
+            VMEM((2, NC, 16, 128), BF16),
+            VMEM((64, 128), F32),
+            DMA((16,)), DMA((10,)), DMA((10,)), DMA((7,)), DMA((7,)),
             DMA((14, 6)), DMA((14, 6)), DMA((8,)), DMA((7,)), DMA((7,)),
+            DMA((8,)), DMA((8,)), DMA((6,)), DMA((6,)),
         ],
         compiler_params=pltpu.CompilerParams(
             collective_id=0, has_side_effects=True, vmem_limit_bytes=62 * 1024 * 1024
         ),
     )(queries, grad_heads, w_uk, w_uv, latents, messages, w_gate, w_up, w_down)
+
+
+def finish_kernel(
+    dq_in, dl_in, kg_in, vg_in, mo_in, wg_in, wu_in, wd_in, select_ref, dest_ref,
+    dq_out, dl_out, kg_out, vg_out, moe_out, gate_out, wg_out, wu_out, wd_out,
+    spread, slots, wg, wu, wd, sem,
+):
+    ins, outs = [], []
+    for n, (src, held, dst) in enumerate(((wg_in, wg, wg_out), (wu_in, wu, wu_out), (wd_in, wd, wd_out))):
+        size = src.shape[0] // 4
+        for k in range(4):
+            part = pl.ds(k * size, size)
+            ins.append(pltpu.make_async_copy(src.at[part], held.at[part], sem.at[4 * n + k]))
+            outs.append(pltpu.make_async_copy(held.at[part], dst.at[part], sem.at[12 + 4 * n + k]))
+    for copy in ins:
+        copy.start()
+    for src, dst in ((dq_in, dq_out), (dl_in, dl_out), (kg_in, kg_out), (vg_in, vg_out)):
+        dst[...] = src[...]
+    for before, after in zip(ins, outs):
+        before.wait()
+        after.start()
+    spread[...] = mo_in[...].reshape(1024, 128).astype(F32)
+
+    def by_slot(row, step):
+        for k in range(CAP):
+            slots[pl.ds(k, 64, stride=2), :] = spread[pl.ds(row + k * step, 64, stride=16), :]
+        return slots[...].astype(BF16)
+
+    select = select_ref[...]
+    twice = jnp.concatenate([select, select], axis=1)
+    for f in range(7):
+        moe_out[:, f * 128 : (f + 1) * 128] = jnp.dot(
+            twice, by_slot(f, 7), preferred_element_type=F32
+        ).astype(BF16)
+    gates = by_slot(14, 1)
+    lane = lax.broadcasted_iota(jnp.int32, (TOK, 128), 1)
+    total = jnp.zeros((TOK, 128), F32)
+    for j in range(8):
+        hit = (dest_ref[:, j : j + 1] == lane % 64).astype(F32).astype(BF16)
+        total = jnp.where(lane == j, jnp.dot(hit, gates, preferred_element_type=F32), total)
+    gate_out[...] = total.T[0:8, :]
+    for copy in outs:
+        copy.wait()
+
+
+def finish(dq, dl, kg, vg, mo, wg, wu, wd, select, dest):
+    anywhere = pl.BlockSpec(memory_space=pl.ANY)
+    whole = pl.BlockSpec(memory_space=VMEM)
+    shape = jax.ShapeDtypeStruct
+    return pl.pallas_call(
+        finish_kernel,
+        out_shape=(
+            shape(dq.shape, BF16),
+            shape(dl.shape, F32),
+            shape(kg.shape, F32),
+            shape(vg.shape, F32),
+            shape((TOK, 896), BF16),
+            shape((8, TOK), F32),
+            shape(wg.shape, BF16),
+            shape(wu.shape, BF16),
+            shape(wd.shape, BF16),
+        ),
+        in_specs=[whole] * 5 + [anywhere] * 3 + [whole] * 2,
+        out_specs=(whole,) * 6 + (anywhere,) * 3,
+        scratch_shapes=[
+            VMEM((1024, 128), F32),
+            VMEM((128, 128), F32),
+            VMEM(wg.shape, BF16),
+            VMEM(wu.shape, BF16),
+            VMEM(wd.shape, BF16),
+            DMA((24,)),
+        ],
+        compiler_params=pltpu.CompilerParams(vmem_limit_bytes=62 * 1024 * 1024),
+    )(dq, dl, kg, vg, mo, wg, wu, wd, select, dest)
 
 
 def on_device(
@@ -680,16 +823,14 @@
         ],
         axis=1,
     )
-    d_queries, d_latents, key_summed, value_summed, returned, gate_wgrad, up_wgrad, down_grad = fused(
+    results = fused(
         queries, grad_heads, w_uk, w_uv, latents, messages, w_gate[0], w_up[0], w_down[0]
     )
-    d_latents = lax.dynamic_slice_in_dim(d_latents, (lax.axis_index("exp") % 2) * 64, 64, 1)
-    moe_grad = jnp.dot(
-        selector, returned[:, :14].reshape(slot_count, 896), precision=lax.Precision.HIGHEST
-    ).astype(BF16)
-    gate_grads = jnp.sum(matches * returned[:, 14:16, 0].reshape(1, 1, slot_count), axis=2)
+    (
+        d_queries, d_latents, key_summed, value_summed, moe_grad, gate_grads, gate_wgrad, up_wgrad, down_grad,
+    ) = finish(*results, selector_low, destination)
     return (
-        d_queries, d_latents, key_summed, value_summed, moe_grad, gate_grads,
+        d_queries, d_latents.T, key_summed, value_summed, moe_grad, gate_grads.T,
         gate_wgrad[None], up_wgrad[None], down_grad[None],
     )
 

time: 158 us -> 134 us (0.85); the launches traced: 155 us -> 134 us
  local copies, waits for them, and re-layouts: 13.8 us -> 1.77 us
  Pallas kernels: 135 us -> 127 us
    pallas_call x1, Pallas kernels: 135 us -> 120 us  [fused(): pl.pallas_call(fused_kernel, out_shape=(shape((TOK, 8 * HD), BF16), shape...]
    unnamed x17 -> x7, local copies, waits for them, and re-layouts: 10 us -> 0.8 us
    pallas_call x0 -> x1, Pallas kernels: none -> 6.98 us  [finish(): pl.pallas_call(finish_kernel, out_shape=(shape(dq.shape, BF16), shape(dl....]
where the time goes in v3:
time: 134 us
  Pallas kernels  127 us (95%)
  other arithmetic  3.11 us (2%)
  local copies, waits for them, and re-layouts  1.77 us (1%)
  matrix products  1.35 us (1%)
    pallas_call x1, Pallas kernels, fused(): pl.pallas_call(fused_kernel, out_shape=(shape((TOK, 8 * HD), BF16), shape...  120 us
    pallas_call x1, Pallas kernels, finish(): pl.pallas_call(finish_kernel, out_shape=(shape(dq.shape, BF16), shape(dl....  6.98 us

profile of v3, /device:TPU:8, one launch (start us, length us, event | category | flops | bytes accessed | tf_op | source)
XLA Modules:
  0.0 133.9 jit_solution(5727064219761605665)
XLA Ops:
  0.6 0.0 copy-start
  0.7 0.1 pad.3.clone
  0.7 0.7 broadcast_compare_fusion
  1.5 0.7 broadcast_multiply_fusion
  2.2 0.7 convert_element_type.29
  2.8 0.1 copy.43
  3.0 0.1 copy.41
  3.1 0.8 copy.42
  3.9 0.0 copy-start.1
  3.9 0.2 convert_reduce_fusion
  4.1 0.1 convert_element_type.31
  4.2 0.1 broadcast_in_dim.25
  4.3 0.1 copy.45.select_ref
  4.4 0.0 copy-done
  4.5 0.0 copy-start.2
  4.5 0.2 convolution_convert_fusion
  4.7 0.1 reshape.34
  4.8 1.1 convolution_convert_fusion.1
  6.0 0.1 reshape.33
  6.1 0.8 maximum_maximum_fusion.moe_ref
  7.0 119.7 %shard_map.196 = (bf16[128,1024]{1,0:T(8,128)(2,1)}, f32[64,128]{1,0:T(8,128)}, f32[16,1024]{1,0:T(8,128)}, f32[16,1024]{1,0:T(8,128)}, bf16[2,32,16,128]{3,2,1,...) custom-call(bf16[128,1024]{1,0:T(8,128)(2,1)} %q_ref.1, ...), custom_call_target="tpu_custom_call" | custom-call | tf_op jit(solution)/shard_map/pallas_call | solution.py:661
  126.7 0.0 copy-done.1
  126.7 0.0 copy-done.2
  126.7 7.0 %shard_map.197 = (bf16[128,1024]{1,0:T(8,128)(2,1)}, f32[64,128]{1,0:T(8,128)}, f32[16,1024]{1,0:T(8,128)}, f32[16,1024]{1,0:T(8,128)}, bf16[128,896]{1,0:T(8,12...) custom-call(bf16[128,1024]{1,0:T(8,128)(2,1)} %get-tuple-element.26., ...), custom_call_target="tpu_custom_call" | custom-call | tf_op jit(solution)/shard_map/pallas_call | solution.py:776
  (3 shorter events, 0.1 us)
Async XLA Ops:
  0.6 3.8 %copy-start = (bf16[128,896]{1,0:T(8,128)(2,1)S(1)}, bf16[128,896]{1,0:T(8,128)(2,1)}, u32[]{:S(2)}) copy-start(bf16[128,896]{1,0:T(8,128)(2,1)} %param.19) | copy-start | bytes 688132
  3.9 122.8 %copy-start.1 = (s32[128,8]{1,0:T(8,128)}, s32[128,8]{1,0:T(8,128)S(1)}, u32[]{:S(2)}) copy-start(s32[128,8]{1,0:T(8,128)S(1)} %add_select_fusion.dest_ref) | copy-start | bytes 12292
  4.5 122.3 %copy-start.2 = (bf16[128,64]{1,0:T(8,128)(2,1)}, bf16[128,64]{1,0:T(8,128)(2,1)S(1)}, u32[]{:S(2)}) copy-start(bf16[128,64]{1,0:T(8,128)(2,1)S(1)} %copy.45.select_ref) | copy-start | bytes 49156

commit v4 on v3

--- a/solution.py
+++ b/solution.py
@@ -102,11 +102,15 @@
     other = (pos + 2) % 4
     before, after = (pos + 3) % 4, (pos + 1) % 4
 
-    def first():
+    def first(ready=lambda q: None):
+        ready(other)
         send(at(other, 0), held.at[0], send_sem.at[0], recv_sem.at[0], right)
         send(at(other, 1), held.at[1], send_sem.at[1], recv_sem.at[1], left)
+        ready(after)
         send(at(after, 1), held.at[3], send_sem.at[2], recv_sem.at[3], right)
+        ready(before)
         send(at(before, 0), held.at[4], send_sem.at[3], recv_sem.at[4], left)
+        ready(pos)
 
     def second():
         drain(held.at[0], recv_sem.at[0])
@@ -137,13 +141,18 @@
     lax.fori_loop(0, dst.shape[0], one, 0)
 
 
+def named_slots(route_ref, slot_ref):
+    slot = slot_ref[...]
+    return jnp.where(slot >= 0, route_ref[...] * CAP + slot, -1).astype(F32).T
+
+
 def fused_kernel(
-    q_ref, g_ref, wk_ref, wv_ref, lat_ref, moe_ref, wg_ref, wu_ref, wd_ref,
+    q_ref, g_ref, wk_ref, wv_ref, lat_ref, x_ref, dy_ref, route_ref, slot_ref, gate_ref, wg_ref, wu_ref, wd_ref,
     dqo, dlo, kgo, vgo, mo, gwgo, gwuo, gwdo,
     lat, lat_t, probs, dprob, tops, o_t, dq_t, dlat, qv, gv, w4, wkv, wvv, dqv, kgv, vgv, kq, kr, ks, kv_held,
     core_out, core_held, part, x_held, y_part, y_held, z_part, z_held,
-    rows, spread, xs, ys, wg, wu, wd, gwg, gwu, gwd, dh, m_part, m_held, m_send, gate_sum,
-    own_sem, send_sem, recv_sem, z_send, z_recv, ring_send, ring_recv, core_sem, last_send, last_recv,
+    rows, spread, xs, ys, wg, wu, wd, gwg, gwu, gwd, dh, m_part, m_held, m_send, gate_sum, moe_ref, by_slot,
+    own_sem, send_sem, recv_sem, z_send, z_recv, ring_send, ring_recv, core_send, core_recv, last_send, last_recv,
     piece_send, piece_recv, local_send, local_recv,
 ):
     at = Place()
@@ -151,6 +160,7 @@
     left_x, right_x = at.ctx(at.z, (at.x + 3) % 4, at.core), at.ctx(at.z, (at.x + 1) % 4, at.core)
     left_y, right_y = at.exp((at.y + 3) % 4, at.zh), at.exp((at.y + 1) % 4, at.zh)
     sibling = at.ctx(at.z, at.x, 1 - at.core)
+    here = at.zh * 4 + at.z
     e_far = at.y * 2 + 1 - at.zh
     greet(
         [at.exp((at.y + k) % 4, at.zh) for k in range(1, 4)],
@@ -181,7 +191,7 @@
         pltpu.make_async_copy(wu_ref, wu, own_sem.at[7]),
         pltpu.make_async_copy(wd_ref, wd, own_sem.at[8]),
     ]
-    for k in (1, 0, 2, 3, 4, 5):
+    for k in range(1, 6):
         own[k].start()
     lat_own = lat.at[at.z, at.x, at.core, :, lanes(at.y)]
     for k in range(1, 4):
@@ -242,6 +252,31 @@
     yb[2]()
     xb[0]()
     piece_b(0, at.x)
+    lane = lax.broadcasted_iota(jnp.int32, (TOK, 128), 1).astype(F32)
+    named = named_slots(route_ref, slot_ref)
+    gate_of = gate_ref[...].astype(F32).T
+    hits = jnp.zeros((TOK, 128), F32)
+    gated = jnp.zeros((TOK, 128), F32)
+    for j in range(8):
+        hit = named[:, j : j + 1] == lane
+        hits = hits + jnp.where(hit, 1.0, 0.0)
+        gated = gated + jnp.where(hit, gate_of[:, j : j + 1], 0.0)
+    hits, gated = hits.astype(BF16), gated.astype(BF16)
+
+    def put(row, step, values):
+        by_slot[...] = values
+        for k in range(CAP):
+            spread[pl.ds(row + k * step, NC, stride=32), :] = by_slot[pl.ds(k, NC, stride=2), :]
+
+    pick = (((0,), (0,)), ((), ()))
+    for f in range(7):
+        cols = slice(f * 128, (f + 1) * 128)
+        put(f, 7, lax.dot_general(hits, x_ref[:, cols], pick, preferred_element_type=F32))
+        put(14 + f, 7, lax.dot_general(hits, dy_ref[:, cols], pick, preferred_element_type=F32))
+    put(28, 1, lax.dot_general(gated, jnp.ones((TOK, 128), BF16), pick, preferred_element_type=F32))
+    put(30, 1, jnp.zeros((128, 128), F32))
+    moe_ref[...] = spread[...].reshape(NC, 32, 128).astype(BF16)
+    own[0].start()
     lax.fori_loop(0, NC - 1, send_rows, 0)
     send(moe_ref.at[c], rows.at[e, c], send_sem.at[9], recv_sem.at[9], (c, e_far))
     ya[1]()
@@ -387,7 +422,6 @@
     class Reduce:
         def __init__(self, b):
             self.b = b
-            self.copy = None
             self.x_ring = scatter_ring(
                 4 + b, at.x, left_x, right_x,
                 lambda q, h: part.at[b, q, pl.ds(64 * h, 64)], x_held.at[b],
@@ -399,23 +433,20 @@
         def to_core(self):
             b = self.b
 
-            def one(x, carry):
+            for k in (2, 1, 3, 0):
+                x = (at.x + k) % 4
                 core_out[b, x] = dlat[self.block(x, 1 - at.core), :].astype(BF16)
-                return carry
-
-            lax.fori_loop(0, 4, one, 0)
-            self.copy = send(core_out.at[b], core_held.at[b], core_sem.at[b], core_sem.at[4 + b], sibling)
+                send(core_out.at[b, x], core_held.at[b, x], core_send.at[b, k], core_recv.at[b, k], sibling)
 
         def x1(self):
             b = self.b
-            self.copy.wait_recv()
-
-            def one(x, carry):
+
+            def ready(x):
+                k = (x + 4 - at.x) % 4
+                drain(core_held.at[b, x], core_recv.at[b, k])
                 part[b, x] = (dlat[self.block(x, at.core), :] + core_held[b, x].astype(F32)).astype(BF16)
-                return carry
-
-            lax.fori_loop(0, 4, one, 0)
-            self.x_ring[0]()
+
+            self.x_ring[0](ready)
 
         def x2(self):
             self.x_ring[1]()
@@ -444,6 +475,14 @@
                 drain(y_held.at[b, k], ring_recv.at[8 + b, k + 1])
                 total = total + y_held[b, k].astype(F32)
             z_part[b] = total.astype(BF16)
+            for half in range(2):
+
+                @pl.when(here != half * 4 + b)
+                def _():
+                    send(
+                        z_part.at[b], z_held.at[here], last_send.at[2 * b + half], last_recv.at[here],
+                        (b * 8 + c % 8, at.y * 2 + half),
+                    )
 
     rs = [Reduce(b) for b in range(4)]
 
@@ -579,56 +618,53 @@
 
     kept = []
 
-    chunk(3, after_output=(rows_here,))
+    chunk(3, after_score=(rows_here,))
     rs[3].to_core()
-    chunk(2, after_score=(rs[3].x1, my[1]), after_output=(rs[3].x2,))
+    my[1]()
+    chunk(2, after_score=(rs[3].x1,), after_output=(rs[3].x2,))
     rs[2].to_core()
-    chunk(1, after_score=(rs[2].x1, rs[3].x3), after_output=(rs[2].x2,))
+    chunk(1, after_score=(rs[2].x1, rs[3].x3, my[2], experts, experts_back, mr[0]), after_output=(rs[2].x2,))
     rs[1].to_core()
+    mr[1]()
     rs[3].y3()
     chunk(0, after_score=(rs[1].x1, rs[2].x3), after_output=(rs[1].x2,))
     rs[0].to_core()
     spread_weights()
-    my[2]()
-    experts()
     rs[0].x1()
+    rows_back()
     rs[2].y3()
     rs[1].x3()
-    experts_back()
-    mr[0]()
     rs[0].x2()
     return_weights()
+    kept.append(down_grads())
+    rs[0].x3()
     rs[1].y3()
-    kept.append(down_grads())
-    mr[1]()
-    rs[0].x3()
     kept.append(weight_grads(gwg, 1, gwgo, own_sem.at[9]))
-    rows_back()
     rs[0].y3()
-    for k in range(1, 8):
-        place = (at.zh * 4 + at.z + k) % 8
-        z = place % 4
-        device = (z * 8 + c % 8, at.y * 2 + place // 4)
-        send(z_part.at[z], z_held.at[k - 1], last_send.at[k - 1], last_recv.at[k - 1], device)
     kept.append(weight_grads(gwu, 2, gwuo, own_sem.at[10]))
-
     drain(ks.at[0], own_sem.at[13])
     drain(ks.at[pl.ds(0, 7)], recv_sem.at[7])
     for n, out in ((0, kgo), (1, vgo)):
         for h in range(8):
             out[:, h * HD : (h + 1) * HD] = kv_held[h, n]
     total = z_part[at.z].astype(F32)
-    for k in range(7):
-        drain(z_held.at[k], last_recv.at[k])
-        total = total + z_held[k].astype(F32)
+    for k in range(1, 8):
+        p = (here + k) % 8
+        drain(z_held.at[p], last_recv.at[p])
+        total = total + z_held[p].astype(F32)
     dlo[...] = jnp.where(at.zh == 0, total[:, :64], total[:, 64:]).T
 
     for copy in kept:
         copy.wait()
-    for k in range(7):
-        drain(z_held.at[k], last_send.at[k])
     for b in range(4):
-        rs[b].copy.wait_send()
+        for half in range(2):
+
+            @pl.when(here != half * 4 + b)
+            def _():
+                drain(z_part.at[b], last_send.at[2 * b + half])
+    for b in range(4):
+        for k in range(4):
+            drain(core_held.at[b, k], core_send.at[b, k])
         for k in range(3):
             drain(y_held.at[b, k], ring_send.at[8 + b, k + 1])
     for k in range(3):
@@ -654,7 +690,7 @@
     drain(ks.at[pl.ds(0, 7)], send_sem.at[7])
 
 
-def fused(queries, grad_heads, w_uk, w_uv, latents, messages, w_gate, w_up, w_down):
+def fused(queries, grad_heads, w_uk, w_uv, latents, moe_in, grad_out, routes, slots, gates, w_gate, w_up, w_down):
     anywhere = pl.BlockSpec(memory_space=pl.ANY)
     whole = pl.BlockSpec(memory_space=VMEM)
     shape = jax.ShapeDtypeStruct
@@ -670,7 +706,7 @@
             shape((7168, 128), BF16),
             shape((128, 7168), BF16),
         ),
-        in_specs=[anywhere] * 9,
+        in_specs=[anywhere] * 5 + [whole] * 5 + [anywhere] * 3,
         out_specs=(anywhere, whole, whole, whole, anywhere, anywhere, anywhere, anywhere),
         scratch_shapes=[
             VMEM((4, 4, 2, TOK, 512), BF16),
@@ -700,7 +736,7 @@
             VMEM((4, 4, TOK, 128), BF16),
             VMEM((4, 3, TOK, 128), BF16),
             VMEM((4, TOK, 128), BF16),
-            VMEM((7, TOK, 128), BF16),
+            VMEM((8, TOK, 128), BF16),
             VMEM((8, NC, 32, 128), BF16),
             VMEM((1024, 128), F32),
             VMEM((64, 7168), BF16),
@@ -716,18 +752,20 @@
             VMEM((6, NC, 16, 128), BF16),
             VMEM((2, NC, 16, 128), BF16),
             VMEM((64, 128), F32),
+            VMEM((NC, 32, 128), BF16),
+            VMEM((128, 128), F32),
             DMA((16,)), DMA((10,)), DMA((10,)), DMA((7,)), DMA((7,)),
-            DMA((14, 6)), DMA((14, 6)), DMA((8,)), DMA((7,)), DMA((7,)),
+            DMA((14, 6)), DMA((14, 6)), DMA((4, 4)), DMA((4, 4)), DMA((8,)), DMA((8,)),
             DMA((8,)), DMA((8,)), DMA((6,)), DMA((6,)),
         ],
         compiler_params=pltpu.CompilerParams(
             collective_id=0, has_side_effects=True, vmem_limit_bytes=62 * 1024 * 1024
         ),
-    )(queries, grad_heads, w_uk, w_uv, latents, messages, w_gate, w_up, w_down)
+    )(queries, grad_heads, w_uk, w_uv, latents, moe_in, grad_out, routes, slots, gates, w_gate, w_up, w_down)
 
 
 def finish_kernel(
-    dq_in, dl_in, kg_in, vg_in, mo_in, wg_in, wu_in, wd_in, select_ref, dest_ref,
+    dq_in, dl_in, kg_in, vg_in, mo_in, wg_in, wu_in, wd_in, route_ref, slot_ref,
     dq_out, dl_out, kg_out, vg_out, moe_out, gate_out, wg_out, wu_out, wd_out,
     spread, slots, wg, wu, wd, sem,
 ):
@@ -752,24 +790,25 @@
             slots[pl.ds(k, 64, stride=2), :] = spread[pl.ds(row + k * step, 64, stride=16), :]
         return slots[...].astype(BF16)
 
-    select = select_ref[...]
-    twice = jnp.concatenate([select, select], axis=1)
+    gates = by_slot(14, 1)
+    number = lax.broadcasted_iota(jnp.int32, (TOK, 128), 1)
+    lane = (number % 64).astype(F32)
+    named = named_slots(route_ref, slot_ref)
+    total = jnp.zeros((TOK, 128), F32)
+    hits = jnp.zeros((TOK, 128), F32)
+    for j in range(8):
+        hit = jnp.where(named[:, j : j + 1] == lane, 1.0, 0.0)
+        hits = hits + hit
+        total = jnp.where(number == j, jnp.dot(hit.astype(BF16), gates, preferred_element_type=F32), total)
+    gate_out[...] = total.T[0:8, :]
+    hits = hits.astype(BF16)
     for f in range(7):
-        moe_out[:, f * 128 : (f + 1) * 128] = jnp.dot(
-            twice, by_slot(f, 7), preferred_element_type=F32
-        ).astype(BF16)
-    gates = by_slot(14, 1)
-    lane = lax.broadcasted_iota(jnp.int32, (TOK, 128), 1)
-    total = jnp.zeros((TOK, 128), F32)
-    for j in range(8):
-        hit = (dest_ref[:, j : j + 1] == lane % 64).astype(F32).astype(BF16)
-        total = jnp.where(lane == j, jnp.dot(hit, gates, preferred_element_type=F32), total)
-    gate_out[...] = total.T[0:8, :]
+        moe_out[:, f * 128 : (f + 1) * 128] = jnp.dot(hits, by_slot(f, 7), preferred_element_type=F32).astype(BF16)
     for copy in outs:
         copy.wait()
 
 
-def finish(dq, dl, kg, vg, mo, wg, wu, wd, select, dest):
+def finish(dq, dl, kg, vg, mo, wg, wu, wd, routes, slots):
     anywhere = pl.BlockSpec(memory_space=pl.ANY)
     whole = pl.BlockSpec(memory_space=VMEM)
     shape = jax.ShapeDtypeStruct
@@ -797,38 +836,20 @@
             DMA((24,)),
         ],
         compiler_params=pltpu.CompilerParams(vmem_limit_bytes=62 * 1024 * 1024),
-    )(dq, dl, kg, vg, mo, wg, wu, wd, select, dest)
+    )(dq, dl, kg, vg, mo, wg, wu, wd, routes, slots)
 
 
 def on_device(
     queries, grad_heads, latents, w_uk, w_uv, moe_in, grad_out, routes, slots, gates, w_gate, w_up, w_down
 ):
-    slot_count = NC * CAP
-    destination = jnp.where(slots >= 0, routes * CAP + slots, -1)
-    matches = (
-        destination[:, :, None] == jnp.arange(slot_count, dtype=jnp.int32)[None, None, :]
-    ).astype(F32)
-    selector = jnp.sum(matches, axis=1)
-    selector_low = selector.astype(BF16)
-    pick = (((0,), (0,)), ((), ()))
-    rows_send = lax.dot_general(selector_low, moe_in, pick, preferred_element_type=F32).astype(BF16)
-    grads_send = lax.dot_general(selector_low, grad_out, pick, preferred_element_type=F32).astype(BF16)
-    gate_send = jnp.sum(matches * gates.astype(F32)[:, :, None], axis=(0, 1)).astype(BF16)
-    messages = jnp.concatenate(
-        [
-            rows_send.reshape(NC, 14, 128),
-            grads_send.reshape(NC, 14, 128),
-            jnp.broadcast_to(gate_send.reshape(NC, CAP, 1), (NC, CAP, 128)),
-            jnp.zeros((NC, 2, 128), BF16),
-        ],
-        axis=1,
-    )
+    routes, slots = routes.T, slots.T
     results = fused(
-        queries, grad_heads, w_uk, w_uv, latents, messages, w_gate[0], w_up[0], w_down[0]
+        queries, grad_heads, w_uk, w_uv, latents, moe_in, grad_out, routes, slots, gates.T,
+        w_gate[0], w_up[0], w_down[0],
     )
     (
         d_queries, d_latents, key_summed, value_summed, moe_grad, gate_grads, gate_wgrad, up_wgrad, down_grad,
-    ) = finish(*results, selector_low, destination)
+    ) = finish(*results, routes, slots)
     return (
         d_queries, d_latents.T, key_summed, value_summed, moe_grad, gate_grads.T,
         gate_wgrad[None], up_wgrad[None], down_grad[None],

time: 134 us -> 130 us (0.970)
  other arithmetic: 3.11 us -> 0 us
  Pallas kernels: 127 us -> 130 us
  local copies, waits for them, and re-layouts: 1.77 us -> 0 us
  matrix products: 1.35 us -> 0 us
    pallas_call x1, Pallas kernels: 120 us -> 123 us  [fused(): pl.pallas_call(fused_kernel, out_shape=(shape((TOK, 8 * HD), BF16), shape...]
    dot_general x2 -> x0, matrix products: 1.35 us -> none  [the longest x1 1.15 us: on_device(): lax.dot_general(selector_low, moe_in, pick, preferred_element_type=F32)]
where the time goes in v4:
time: 130 us
  Pallas kernels  130 us (100%)
    pallas_call x1, Pallas kernels, fused(): pl.pallas_call(fused_kernel, out_shape=(shape((TOK, 8 * HD), BF16), shape...  123 us
    pallas_call x1, Pallas kernels, finish(): pl.pallas_call(finish_kernel, out_shape=(shape(dq.shape, BF16), shape(dl....  6.98 us

profile of v4, /device:TPU:8, one launch (start us, length us, event | category | flops | bytes accessed | tf_op | source)
XLA Modules:
  0.0 130.3 jit_solution(2692253021343690363)
XLA Ops:
  0.6 122.5 %shard_map.196 = (bf16[128,1024]{1,0:T(8,128)(2,1)}, f32[64,128]{1,0:T(8,128)}, f32[16,1024]{1,0:T(8,128)}, f32[16,1024]{1,0:T(8,128)}, bf16[2,32,16,128]{3,2,1,...) custom-call(bf16[128,1024]{1,0:T(8,128)(2,1)} %q_ref.1, ...), custom_call_target="tpu_custom_call" | custom-call | tf_op jit(solution)/shard_map/pallas_call | solution.py:697
  123.2 7.0 %shard_map.197 = (bf16[128,1024]{1,0:T(8,128)(2,1)}, f32[64,128]{1,0:T(8,128)}, f32[16,1024]{1,0:T(8,128)}, f32[16,1024]{1,0:T(8,128)}, bf16[128,896]{1,0:T(8,12...) custom-call(bf16[128,1024]{1,0:T(8,128)(2,1)} %get-tuple-element.26., ...), custom_call_target="tpu_custom_call" | custom-call | tf_op jit(solution)/shard_map/pallas_call | solution.py:815
